TPU v7x, 32 devices: a whole 2x2x4 slice. The times are simulated.
32 devices in a mesh: dp: 2 (over x), wide: 16 (over z, y, core).
Axes of the slice: x: 2, y: 2, z: 4, core: 2. Of those that a mesh axis runs over, the one named last changes fastest.
Arguments:
- tokens: bfloat16 [4, 1024, 2048], P('dp', 'wide'), may hold values from -6 to 6
- lengths: int32 [4], P('dp'), may hold values from 128 to 1024, as said below
- gain_one: bfloat16 [2048], P('wide'), may hold values from 0.5 to 1.5
- shift_one: bfloat16 [2048], P('wide'), may hold values from -1 to 1
- w_qkv: bfloat16 [2048, 6144], P('wide'), may hold values from -0.125 to 0.125
- b_qkv: bfloat16 [6144], P('wide'), may hold values from -1 to 1
- w_dense: bfloat16 [2048, 2048], P('wide'), may hold values from -0.5 to 0.5
- b_dense: bfloat16 [2048], P('wide'), may hold values from -1 to 1
- gain_two: bfloat16 [2048], P('wide'), may hold values from 0.5 to 1.5
- shift_two: bfloat16 [2048], P('wide'), may hold values from -1 to 1
- w_up: bfloat16 [2048, 8192], P('wide'), may hold values from -0.125 to 0.125
- b_up: bfloat16 [8192], P('wide'), may hold values from -1 to 1
- w_down: bfloat16 [8192, 2048], P('wide'), may hold values from -0.0625 to 0.0625
- b_down: bfloat16 [2048], P('wide'), may hold values from -1 to 1
- cotangent: bfloat16 [4, 1024, 2048], P('dp', 'wide'), may hold values from -6 to 6
Outputs:
- mixed: bfloat16 [4, 1024, 2048], P('dp', 'wide')
- token_grad: bfloat16 [4, 1024, 2048], P('dp', 'wide')
- grad_gain_one: float32 [2048], P('wide')
- grad_shift_one: float32 [2048], P('wide')
- grad_w_qkv: float32 [2048, 6144], P('wide')
- grad_b_qkv: float32 [6144], P('wide')
- grad_w_dense: float32 [2048, 2048], P('wide')
- grad_b_dense: float32 [2048], P('wide')
- grad_gain_two: float32 [2048], P('wide')
- grad_shift_two: float32 [2048], P('wide')
- grad_w_up: float32 [2048, 8192], P('wide')
- grad_b_up: float32 [8192], P('wide')
- grad_w_down: float32 [8192, 2048], P('wide')
- grad_b_down: float32 [2048], P('wide')
Inputs may be any that keep to these rules, and one draw needn't show every extreme that they name: `lengths`: in each group of 2 sequences [i * 2, (i + 1) * 2) one has length exactly 1024; exactly one sequence of all has length 128.
All inputs are finite; a program needn't handle non-finite values.
Results may differ from a plain program's by a relative error of at most 0.0092.
Values may be sent and summed in bfloat16 or wider, within the bound.
No kernel may reach another device: no remote copies, remote signals or barrier semaphores. Data moves between devices by JAX's collectives and lax.ppermute only.
A program may use at most 640 MiB of HBM per device.

v0:
```python
import jax
import jax.numpy as jnp
from jax import lax
from jax.sharding import PartitionSpec as P

HEADS = 8
HEAD_DIM = 256
ROT = 64


EPS = 1e-05
MASKED = -1e30
ROT_BASE = 10000.0
ROOT_HALF = 0.7071067811865476


def gelu_exact(values):
    return 0.5 * values * (1.0 + jax.scipy.special.erf(values * ROOT_HALF))


def norm_core(values, gain_vec):
    average = jnp.mean(values, axis=-1, keepdims=True)
    centered = values - average
    variance = jnp.mean(centered * centered, axis=-1, keepdims=True)
    return centered * lax.rsqrt(variance + EPS) * gain_vec


def rotary_tables(places):
    halves = ROT // 2
    inverse = ROT_BASE ** (-2.0 * jnp.arange(halves, dtype=jnp.float32) / ROT)
    angles = places.astype(jnp.float32)[:, None] * inverse[None, :]
    return (jnp.cos(angles), jnp.sin(angles))


def rotate(head_rows, cosine, sine_table):
    halves = ROT // 2
    first = head_rows[..., :halves]
    second = head_rows[..., halves:ROT]
    cosine_col = cosine[:, None, :]
    sine_col = sine_table[:, None, :]
    return jnp.concatenate(
        [
            first * cosine_col - second * sine_col,
            second * cosine_col + first * sine_col,
            head_rows[..., ROT:],
        ],
        axis=-1,
    )


def soft_pair(query_blk, grad_blk, total_blk, key_blk, value_blk, allowed, score_scale):
    raw_scores = (
        jnp.einsum("qhd,khd->hqk", query_blk, key_blk, preferred_element_type=jnp.float32)
        * score_scale
    )
    soft_probs = jnp.exp(jnp.where(allowed[None], raw_scores, MASKED) - total_blk[..., None])
    grad_soft = jnp.einsum("qhd,khd->hqk", grad_blk, value_blk, preferred_element_type=jnp.float32)
    return (soft_probs, grad_soft)


def key_terms(query_blk, grad_blk, total_blk, delta_blk, key_blk, value_blk, allowed, score_scale):
    soft_probs, grad_soft = soft_pair(
        query_blk, grad_blk, total_blk, key_blk, value_blk, allowed, score_scale
    )
    grad_scores = (soft_probs * (grad_soft - delta_blk[..., None])).astype(jnp.bfloat16)
    grad_key = (
        jnp.einsum("hqk,qhd->khd", grad_scores, query_blk, preferred_element_type=jnp.float32)
        * score_scale
    )
    grad_value = jnp.einsum(
        "hqk,qhd->khd",
        soft_probs.astype(jnp.bfloat16),
        grad_blk,
        preferred_element_type=jnp.float32,
    )
    return (grad_key, grad_value)


def local(
    tokens,
    lengths,
    gain_one,
    shift_one,
    w_qkv,
    b_qkv,
    w_dense,
    b_dense,
    gain_two,
    shift_two,
    w_up,
    b_up,
    w_down,
    b_down,
    cotangent,
):
    seq_count, span_len, model_width = tokens.shape
    wide_count = lax.axis_size("wide")
    full_len = span_len * wide_count
    row_count = seq_count * span_len
    places = lax.axis_index("wide") * span_len + jnp.arange(span_len, dtype=jnp.int32)
    all_places = jnp.arange(full_len, dtype=jnp.int32)
    valid_rows = (places[None, :] < lengths[:, None]).astype(jnp.float32).reshape(row_count, 1)
    cosine, sine_table = rotary_tables(places)
    score_scale = HEAD_DIM ** (-0.5)
    f32 = jnp.float32
    bf16 = jnp.bfloat16
    (
        full_gain_one,
        full_shift_one,
        full_w_qkv,
        full_b_qkv,
        full_w_dense,
        full_b_dense,
        full_gain_two,
        full_shift_two,
        full_w_up,
        full_b_up,
        full_w_down,
        full_b_down,
    ) = (
        lax.all_gather(gain_one, "wide", axis=0, tiled=True),
        lax.all_gather(shift_one, "wide", axis=0, tiled=True),
        lax.all_gather(w_qkv, "wide", axis=0, tiled=True),
        lax.all_gather(b_qkv, "wide", axis=0, tiled=True),
        lax.all_gather(w_dense, "wide", axis=0, tiled=True),
        lax.all_gather(b_dense, "wide", axis=0, tiled=True),
        lax.all_gather(gain_two, "wide", axis=0, tiled=True),
        lax.all_gather(shift_two, "wide", axis=0, tiled=True),
        lax.all_gather(w_up, "wide", axis=0, tiled=True),
        lax.all_gather(b_up, "wide", axis=0, tiled=True),
        lax.all_gather(w_down, "wide", axis=0, tiled=True),
        lax.all_gather(b_down, "wide", axis=0, tiled=True),
    )
    flat_in = tokens.reshape(row_count, model_width).astype(f32)
    normed_one_low = (
        norm_core(flat_in, full_gain_one.astype(f32)) + full_shift_one.astype(f32)
    ).astype(bf16)
    joined_qkv = jnp.dot(
        normed_one_low, full_w_qkv, preferred_element_type=f32
    ) + full_b_qkv.astype(f32)
    split_heads = joined_qkv.reshape(seq_count, span_len, 3, HEADS, HEAD_DIM)
    queries = rotate(split_heads[:, :, 0], cosine, sine_table).astype(bf16)
    key_heads = rotate(split_heads[:, :, 1], cosine, sine_table).astype(bf16)
    value_heads = split_heads[:, :, 2].astype(bf16)
    key_all, value_all = (
        lax.all_gather(
            key_heads.reshape(seq_count, span_len, model_width), "wide", axis=1, tiled=True
        ),
        lax.all_gather(
            value_heads.reshape(seq_count, span_len, model_width), "wide", axis=1, tiled=True
        ),
    )

    def attend_one(packed):
        query_seq, key_seq, value_seq, length = packed
        allowed = (all_places[None, :] <= places[:, None]) & (all_places[None, :] < length)
        raw_scores = (
            jnp.einsum(
                "qhd,khd->hqk",
                query_seq,
                key_seq.reshape(full_len, HEADS, HEAD_DIM),
                preferred_element_type=f32,
            )
            * score_scale
        )
        masked = jnp.where(allowed[None], raw_scores, MASKED)
        highest = jnp.max(masked, axis=-1, keepdims=True)
        raised = jnp.exp(masked - highest)
        totals = jnp.sum(raised, axis=-1, keepdims=True)
        soft_probs = (raised / totals).astype(bf16)
        attended = jnp.einsum(
            "hqk,khd->qhd",
            soft_probs,
            value_seq.reshape(full_len, HEADS, HEAD_DIM),
            preferred_element_type=f32,
        )
        return (
            attended.reshape(span_len, model_width).astype(bf16),
            (highest + jnp.log(totals))[..., 0],
        )

    attended_low, log_totals = lax.map(attend_one, (queries, key_all, value_all, lengths))
    attended_flat = attended_low.reshape(row_count, model_width)
    branch_attn = jnp.dot(
        attended_flat, full_w_dense, preferred_element_type=f32
    ) + full_b_dense.astype(f32)
    normed_two_low = (
        norm_core(flat_in, full_gain_two.astype(f32)) + full_shift_two.astype(f32)
    ).astype(bf16)
    upper_in = jnp.dot(normed_two_low, full_w_up, preferred_element_type=f32) + full_b_up.astype(
        f32
    )
    activated_low = gelu_exact(upper_in).astype(bf16)
    branch_mlp = jnp.dot(
        activated_low, full_w_down, preferred_element_type=f32
    ) + full_b_down.astype(f32)
    mixed = (
        (valid_rows * (flat_in + branch_attn + branch_mlp))
        .astype(bf16)
        .reshape(seq_count, span_len, model_width)
    )
    back_gain_one, back_gain_two, back_w_qkv, back_w_dense, back_w_up, back_w_down = (
        lax.all_gather(gain_one, "wide", axis=0, tiled=True),
        lax.all_gather(gain_two, "wide", axis=0, tiled=True),
        lax.all_gather(w_qkv, "wide", axis=0, tiled=True),
        lax.all_gather(w_dense, "wide", axis=0, tiled=True),
        lax.all_gather(w_up, "wide", axis=0, tiled=True),
        lax.all_gather(w_down, "wide", axis=0, tiled=True),
    )
    grad_out = cotangent.reshape(row_count, model_width).astype(f32) * valid_rows
    grad_out_low = grad_out.astype(bf16)
    bias_grad_out = jnp.sum(grad_out, axis=0)
    grad_w_down = jnp.einsum("rf,rd->fd", activated_low, grad_out_low, preferred_element_type=f32)
    grad_w_dense = jnp.einsum("re,rd->ed", attended_flat, grad_out_low, preferred_element_type=f32)
    grad_activated = jnp.einsum("rd,fd->rf", grad_out_low, back_w_down, preferred_element_type=f32)
    gelu_value, gelu_pull = jax.vjp(gelu_exact, upper_in)
    grad_upper_low = gelu_pull(grad_activated)[0].astype(bf16)
    grad_b_up = jnp.sum(grad_upper_low.astype(f32), axis=0)
    grad_w_up = jnp.einsum("rd,rf->df", normed_two_low, grad_upper_low, preferred_element_type=f32)
    grad_normed_two = jnp.einsum("rf,df->rd", grad_upper_low, back_w_up, preferred_element_type=f32)
    norm_value_two, norm_pull_two = jax.vjp(norm_core, flat_in, back_gain_two.astype(f32))
    grad_x_two, grad_gain_two = norm_pull_two(grad_normed_two)
    grad_shift_two = jnp.sum(grad_normed_two, axis=0)
    grad_attended_low = jnp.einsum(
        "re,de->rd", grad_out_low, back_w_dense, preferred_element_type=f32
    ).astype(bf16)
    grad_heads = grad_attended_low.reshape(seq_count, span_len, HEADS, HEAD_DIM)

    def query_side(packed):
        query_seq, key_seq, value_seq, grad_seq, total_seq, length = packed
        allowed = (all_places[None, :] <= places[:, None]) & (all_places[None, :] < length)
        key_blk = key_seq.reshape(full_len, HEADS, HEAD_DIM)
        soft_probs, grad_soft = soft_pair(
            query_seq,
            grad_seq,
            total_seq,
            key_blk,
            value_seq.reshape(full_len, HEADS, HEAD_DIM),
            allowed,
            score_scale,
        )
        deltas = jnp.sum(soft_probs * grad_soft, axis=-1)
        grad_scores = (soft_probs * (grad_soft - deltas[..., None])).astype(bf16)
        grad_query = (
            jnp.einsum("hqk,khd->qhd", grad_scores, key_blk, preferred_element_type=f32)
            * score_scale
        )
        return (grad_query, deltas)

    grad_queries, deltas = lax.map(
        query_side, (queries, key_all, value_all, grad_heads, log_totals, lengths)
    )
    query_all, grad_all = (
        lax.all_gather(
            queries.reshape(seq_count, span_len, model_width), "wide", axis=1, tiled=True
        ),
        lax.all_gather(
            grad_attended_low.reshape(seq_count, span_len, model_width), "wide", axis=1, tiled=True
        ),
    )
    total_all, delta_all = (
        lax.all_gather(log_totals, "wide", axis=2, tiled=True),
        lax.all_gather(deltas, "wide", axis=2, tiled=True),
    )

    def own_keys(packed):
        query_seq, grad_seq, total_seq, delta_seq, key_seq, value_seq, length = packed
        allowed = (places[None, :] <= all_places[:, None]) & (places[None, :] < length)
        grad_key, grad_value = key_terms(
            query_seq.reshape(full_len, HEADS, HEAD_DIM),
            grad_seq.reshape(full_len, HEADS, HEAD_DIM),
            total_seq,
            delta_seq,
            key_seq,
            value_seq,
            allowed,
            score_scale,
        )
        return jnp.concatenate(
            [grad_key.reshape(span_len, model_width), grad_value.reshape(span_len, model_width)],
            axis=-1,
        )

    own_grads = lax.map(
        own_keys, (query_all, grad_all, total_all, delta_all, key_heads, value_heads, lengths)
    )
    grad_key_own = own_grads[..., :model_width].reshape(seq_count, span_len, HEADS, HEAD_DIM)
    grad_value_own = own_grads[..., model_width:].reshape(seq_count, span_len, HEADS, HEAD_DIM)
    grad_query_pre = rotate(grad_queries, cosine, -sine_table)
    grad_key_pre = rotate(grad_key_own, cosine, -sine_table)
    grad_joined_low = (
        jnp.stack([grad_query_pre, grad_key_pre, grad_value_own], axis=2)
        .reshape(row_count, 3 * model_width)
        .astype(bf16)
    )
    grad_b_qkv = jnp.sum(grad_joined_low.astype(f32), axis=0)
    grad_w_qkv = jnp.einsum(
        "rd,re->de", normed_one_low, grad_joined_low, preferred_element_type=f32
    )
    grad_normed_one = jnp.einsum(
        "re,de->rd", grad_joined_low, back_w_qkv, preferred_element_type=f32
    )
    norm_value_one, norm_pull_one = jax.vjp(norm_core, flat_in, back_gain_one.astype(f32))
    grad_x_one, grad_gain_one = norm_pull_one(grad_normed_one)
    grad_shift_one = jnp.sum(grad_normed_one, axis=0)
    token_grad = (
        (grad_out + grad_x_one + grad_x_two).astype(bf16).reshape(seq_count, span_len, model_width)
    )
    (
        part_gain_one,
        part_shift_one,
        part_w_qkv,
        part_b_qkv,
        part_w_dense,
        part_b_dense,
        part_gain_two,
        part_shift_two,
        part_w_up,
        part_b_up,
        part_w_down,
        part_b_down,
    ) = (
        lax.psum_scatter(grad_gain_one, "wide", scatter_dimension=0, tiled=True),
        lax.psum_scatter(grad_shift_one, "wide", scatter_dimension=0, tiled=True),
        lax.psum_scatter(grad_w_qkv, "wide", scatter_dimension=0, tiled=True),
        lax.psum_scatter(grad_b_qkv, "wide", scatter_dimension=0, tiled=True),
        lax.psum_scatter(grad_w_dense, "wide", scatter_dimension=0, tiled=True),
        lax.psum_scatter(bias_grad_out, "wide", scatter_dimension=0, tiled=True),
        lax.psum_scatter(grad_gain_two, "wide", scatter_dimension=0, tiled=True),
        lax.psum_scatter(grad_shift_two, "wide", scatter_dimension=0, tiled=True),
        lax.psum_scatter(grad_w_up, "wide", scatter_dimension=0, tiled=True),
        lax.psum_scatter(grad_b_up, "wide", scatter_dimension=0, tiled=True),
        lax.psum_scatter(grad_w_down, "wide", scatter_dimension=0, tiled=True),
        lax.psum_scatter(bias_grad_out, "wide", scatter_dimension=0, tiled=True),
    )
    summed = (
        lax.psum(part_gain_one.astype(jnp.bfloat16), "dp").astype(jnp.float32),
        lax.psum(part_shift_one.astype(jnp.bfloat16), "dp").astype(jnp.float32),
        lax.psum(part_w_qkv.astype(jnp.bfloat16), "dp").astype(jnp.float32),
        lax.psum(part_b_qkv.astype(jnp.bfloat16), "dp").astype(jnp.float32),
        lax.psum(part_w_dense.astype(jnp.bfloat16), "dp").astype(jnp.float32),
        lax.psum(part_b_dense.astype(jnp.bfloat16), "dp").astype(jnp.float32),
        lax.psum(part_gain_two.astype(jnp.bfloat16), "dp").astype(jnp.float32),
        lax.psum(part_shift_two.astype(jnp.bfloat16), "dp").astype(jnp.float32),
        lax.psum(part_w_up.astype(jnp.bfloat16), "dp").astype(jnp.float32),
        lax.psum(part_b_up.astype(jnp.bfloat16), "dp").astype(jnp.float32),
        lax.psum(part_w_down.astype(jnp.bfloat16), "dp").astype(jnp.float32),
        lax.psum(part_b_down.astype(jnp.bfloat16), "dp").astype(jnp.float32),
    )
    return (
        mixed,
        token_grad,
        summed[0],
        summed[1],
        summed[2],
        summed[3],
        summed[4],
        summed[5],
        summed[6],
        summed[7],
        summed[8],
        summed[9],
        summed[10],
        summed[11],
    )


def solution(mesh):
    in_specs = (
        P("dp", "wide", None),
        P("dp"),
        P("wide"),
        P("wide"),
        P("wide", None),
        P("wide"),
        P("wide", None),
        P("wide"),
        P("wide"),
        P("wide"),
        P("wide", None),
        P("wide"),
        P("wide", None),
        P("wide"),
        P("dp", "wide", None),
    )
    out_specs = (
        P("dp", "wide", None),
        P("dp", "wide", None),
        P("wide"),
        P("wide"),
        P("wide", None),
        P("wide"),
        P("wide", None),
        P("wide"),
        P("wide"),
        P("wide"),
        P("wide", None),
        P("wide"),
        P("wide", None),
        P("wide"),
    )
    return jax.shard_map(local, mesh=mesh, in_specs=in_specs, out_specs=out_specs, check_vma=False)
```

profile of v0, /device:TPU:0, one launch (start us, length us, event | category | flops | bytes accessed | tf_op | source)
XLA Modules:
  0.0 2974.0 jit_solution(5575470710544261611)
XLA Ops:
  8.7 23.2 all-gather.5
  52.2 18.9 all-gather.1
  89.3 19.2 all-gather.2
  110.9 30.3 %all-gather.17.cloned.1.call-done = bf16[2048,6144]{1,0:T(8,128)(2,1)} async-done(((bf16[128,6144]{1,0:T(8,128)(2,1)}), bf16[2048,6144]{1,0:T(8,128)(2,1)}) %all-gather.17.cloned.1.call-update) | async-done | bytes 25165840 | tf_op jit(solution)/shard_map/all_gather | solution.py:123
  162.5 56.0 %all-gather.23.cloned.1.call-done = bf16[2048,2048]{1,0:T(8,128)(2,1)} async-done(((bf16[128,2048]{1,0:T(8,128)(2,1)}), bf16[2048,2048]{1,0:T(8,128)(2,1)}) %all-gather.23.cloned.1.call-update) | async-done | bytes 8388624 | tf_op jit(solution)/shard_map/all_gather | solution.py:125
  229.9 64.6 %all-gather.19.cloned.1.call-done = bf16[2,1024,2048]{2,0,1:T(2,128)(2,1)} async-done(((bf16[2,64,2048]{2,0,1:T(2,128)(2,1)}), bf16[2,1024,2048]{2,0,1:T(2,128)(2,1)}) %all-gather.19.cloned.1.call-update) | async-done | bytes 8388624 | tf_op jit(solution)/shard_map/all_gather | solution.py:149
  294.4 21.3 copy.76
  315.7 54.6 %all-gather.21.cloned.1.call-done = bf16[2,1024,2048]{2,1,0:T(8,128)(2,1)} async-done(((bf16[2,64,2048]{2,1,0:T(8,128)(2,1)}), bf16[2,1024,2048]{2,1,0:T(8,128)(2,1)}) %all-gather.21.cloned.1.call-update) | async-done | bytes 8388624 | tf_op jit(solution)/shard_map/all_gather | solution.py:146
  382.2 18.6 while.40
  412.1 33.3 %all-gather.31.cloned.1.call-done = bf16[2,1024,2048]{2,0,1:T(2,128)(2,1)} async-done(((bf16[2,64,2048]{2,0,1:T(2,128)(2,1)}), bf16[2,1024,2048]{2,0,1:T(2,128)(2,1)}) %all-gather.31.cloned.1.call-update) | async-done | bytes 8388624 | tf_op jit(solution)/shard_map/all_gather | solution.py:257
  445.5 21.3 copy.92
  467.7 25.9 all_gather.75
  494.0 19.6 while.41
  513.8 23.6 all_gather.77
  537.9 58.8 %while.39 = (s32[]{:T(128)}, f32[2,64,4096]{2,1,0:T(8,128)}, bf16[2,1024,2048]{2,1,0:T(8,128)(2,1)}, s32[2]{0:T(128)S(1)}, bf16[2,64,8,256]{3,2,1,0:T(8,128)(2,1...) while((s32[]{:T(128)}, f32[2,64,4096]{2,1,0:T(8,128)}, ...), condition=%wide.region_10.11_spmd.clone, body=%wide.region_9.10_spmd.clone.sunk | while | flops 1077936384 | bytes 105186128 | solution.py:284
  603.0 21.5 fusion.66
  625.2 19.8 all-gather.6
  645.0 51.0 %all-gather.25.cloned.1.call-done = bf16[2048,8192]{1,0:T(8,128)(2,1)} async-done(((bf16[128,8192]{1,0:T(8,128)(2,1)}), bf16[2048,8192]{1,0:T(8,128)(2,1)}) %all-gather.25.cloned.1.call-update) | async-done | bytes 33554448 | tf_op jit(solution)/shard_map/all_gather | solution.py:129
  696.0 18.5 convolution_add_fusion
  714.5 151.0 %all-gather.27.cloned.1.call-done = bf16[8192,2048]{1,0:T(8,128)(2,1)} async-done(((bf16[512,2048]{1,0:T(8,128)(2,1)}), bf16[8192,2048]{1,0:T(8,128)(2,1)}) %all-gather.27.cloned.1.call-update) | async-done | bytes 33554448 | tf_op jit(solution)/shard_map/all_gather | solution.py:131
  865.5 20.5 convert_reduce_fusion
  886.0 28.1 fusion.67
  914.4 26.2 fusion.62
  941.3 21.5 all-gather.3
  962.7 18.0 all-gather.7
  983.6 17.6 fusion.65
  1001.2 47.1 %reduce-scatter.7.cloned.1.call-done = f32[128,2048]{1,0:T(8,128)} async-done(((f32[2048,2048]{1,0:T(8,128)}), f32[128,2048]{1,0:T(8,128)}) %reduce-scatter.7.cloned.1.call-update) | async-done | bytes 1048592 | tf_op jit(solution)/shard_map/reduce_scatter | solution.py:327
  1050.3 468.9 %reduce-scatter.5.cloned.1.call-done = f32[128,6144]{1,0:T(8,128)} async-done(((f32[2048,6144]{1,0:T(8,128)}), f32[128,6144]{1,0:T(8,128)}) %reduce-scatter.5.cloned.1.call-update) | async-done | bytes 3145744 | tf_op jit(solution)/shard_map/reduce_scatter | solution.py:325
  1522.4 637.1 %reduce-scatter.9.cloned.1.call-done = f32[128,8192]{1,0:T(8,128)} async-done(((f32[2048,8192]{1,0:T(8,128)}), f32[128,8192]{1,0:T(8,128)}) %reduce-scatter.9.cloned.1.call-update) | async-done | bytes 4194320 | tf_op jit(solution)/shard_map/reduce_scatter | solution.py:331
  2163.3 636.4 %reduce-scatter.11.cloned.1.call-done = f32[512,2048]{1,0:T(8,128)} async-done(((f32[8192,2048]{1,0:T(8,128)}), f32[512,2048]{1,0:T(8,128)}) %reduce-scatter.11.cloned.1.call-update) | async-done | bytes 4194320 | tf_op jit(solution)/shard_map/reduce_scatter | solution.py:333
  2822.9 59.8 %all-reduce.7 = (bf16[2048]{0:T(1024)(128)(2,1)S(1)}, bf16[2048]{0:T(1024)(128)(2,1)S(1)}, bf16[6144]{0:T(1024)(128)(2,1)S(1)}, bf16[2048]{0:T(1024)(128)(2,1)S(...) all-reduce(f32[2048]{0:T(1024)S(1)} %get-tuple-element.379, ...), channel_id=2, replica_groups=mesh['dp'=2,'wide'=16] {'wide'}, use_global_device_ids=true, to_apply=%region_16.17.clone | all-reduce | flops 24576 | bytes 147456
  2915.1 41.8 %all-reduce.12.cloned.1.call-done = (bf16[128,6144]{1,0:T(8,128)(2,1)}, bf16[128,2048]{1,0:T(8,128)(2,1)}, bf16[128,8192]{1,0:T(8,128)(2,1)}, bf16[512,2048]{1,0:T(8,128)(2,1)}) async-done(((bf16[128,6144]{1,0:T(8,128)(2,1)}, bf16[128,2048]{1,0:T(8,128)(2,1)}, bf16[128,8192]{1,0:T(8,128)(2,1)}, bf16[512,2048]{1,0:T(8,128)(2,1)}), (bf16[128,6144]{1,0:T(8,128)(2,1)}, bf16[128,2048]{1,0:T(8,128)(2,1)}, ...) | async-done | bytes 6291472 | tf_op jit(solution)/shard_map/psum | solution.py:339
  (302 shorter events, 279.8 us)
Async XLA Ops:
  7.2 134.0 %all-gather.17.cloned.1.call-start = ((), (), s32[]{:S(2)}) async-start(), calls=%async_computation.4 | async-start | bytes 26738688 | tf_op jit(solution)/shard_map/all_gather | solution.py:123
  7.9 210.6 %all-gather.23.cloned.1.call-start = ((), (), s32[]{:S(2)}) async-start(), calls=%async_computation.7 | async-start | bytes 8912896 | tf_op jit(solution)/shard_map/all_gather | solution.py:125
  8.7 285.8 %all-gather.19.cloned.1.call-start = ((), (), s32[]{:S(2)}) async-start(), calls=%async_computation.5 | async-start | bytes 8912896 | tf_op jit(solution)/shard_map/all_gather | solution.py:149
  49.4 101.7 %copy-start.25 = (f32[16,1,128]{2,1,0:T(1,128)}, f32[16,1,128]{2,1,0:T(1,128)S(1)}, u32[]{:S(2)}) copy-start(f32[16,1,128]{2,1,0:T(1,128)S(1)} %convert_element_type.314) | copy-start | bytes 24580
  50.7 100.4 %copy-start.30 = (f32[128]{0:T(128)}, f32[128]{0:T(128)S(1)}, u32[]{:S(2)}) copy-start(f32[128]{0:T(128)S(1)} %div.50) | copy-start | bytes 1540
  52.1 36.4 %copy-start.40 = (f32[128]{0:T(128)}, f32[128]{0:T(128)S(1)}, u32[]{:S(2)}) copy-start(f32[128]{0:T(128)S(1)} %add.187) | copy-start | bytes 1540
  52.2 99.0 %copy-start.34 = (f32[128]{0:T(128)}, f32[128]{0:T(128)S(1)}, u32[]{:S(2)}) copy-start(f32[128]{0:T(128)S(1)} %rsqrt.18) | copy-start | bytes 1540
  88.6 321.3 %copy-start.21 = (f32[16,1,128]{2,1,0:T(1,128)}, f32[16,1,128]{2,1,0:T(1,128)S(1)}, u32[]{:S(2)}) copy-start(f32[16,1,128]{2,1,0:T(1,128)S(1)} %convert_element_type.310) | copy-start | bytes 24580
  156.2 214.0 %all-gather.21.cloned.1.call-start = ((), (), s32[]{:S(2)}) async-start(), calls=%async_computation.6 | async-start | bytes 8912896 | tf_op jit(solution)/shard_map/all_gather | solution.py:146
  162.1 283.4 %all-gather.31.cloned.1.call-start = ((), (), s32[]{:S(2)}) async-start(), calls=%async_computation.11 | async-start | bytes 8912896 | tf_op jit(solution)/shard_map/all_gather | solution.py:257
  162.2 238.5 %copy-start.28 = (f32[2,64]{1,0:T(2,128)}, f32[2,64]{1,0:T(2,128)S(1)}, u32[]{:S(2)}) copy-start(f32[2,64]{1,0:T(2,128)S(1)} %compare_convert_fusion) | copy-start | bytes 1540
  162.3 62.5 %copy-start.32 = (f32[128]{0:T(128)}, f32[128]{0:T(128)S(1)}, u32[]{:S(2)}) copy-start(f32[128]{0:T(128)S(1)} %reshape.505) | copy-start | bytes 1540
  162.5 62.3 %copy-start.10 = (bf16[128,2048]{1,0:T(8,128)(2,1)}, bf16[128,2048]{1,0:T(8,128)(2,1)S(1)}, u32[]{:S(2)}) copy-start(bf16[128,2048]{1,0:T(8,128)(2,1)S(1)} %fusion.51) | copy-start | bytes 1572868
  162.5 63.7 %copy-start.8 = (f32[2,64,8,256]{3,2,1,0:T(8,128)S(1)}, f32[2,64,8,256]{3,2,1,0:T(8,128)}, u32[]{:S(2)}) copy-start(f32[2,64,8,256]{3,2,1,0:T(8,128)} %copy-done.7) | copy-start | bytes 3145732
  226.2 311.7 %all-gather.29.cloned.1.call-start = ((), (), s32[]{:S(2)}) async-start(), calls=%async_computation.10 | async-start | bytes 8912896 | tf_op jit(solution)/shard_map/all_gather | solution.py:254
  228.0 468.0 %all-gather.25.cloned.1.call-start = ((), (), s32[]{:S(2)}) async-start(), calls=%async_computation.8 | async-start | bytes 35651584 | tf_op jit(solution)/shard_map/all_gather | solution.py:129
  228.7 636.7 %all-gather.27.cloned.1.call-start = ((), (), s32[]{:S(2)}) async-start(), calls=%async_computation.9 | async-start | bytes 35651584 | tf_op jit(solution)/shard_map/all_gather | solution.py:131
  229.5 818.7 %reduce-scatter.7.cloned.1.call-start = ((), (), s32[]{:S(2)}) async-start(), calls=%async_computation.13 | async-start | bytes 17825792 | tf_op jit(solution)/shard_map/reduce_scatter | solution.py:327
  409.8 1109.3 %reduce-scatter.5.cloned.1.call-start = ((), (), s32[]{:S(2)}) async-start(), calls=%async_computation.12 | async-start | bytes 53477376 | tf_op jit(solution)/shard_map/reduce_scatter | solution.py:325
  412.1 54.6 %copy-start.13 = (bf16[2,64,1,8,256]{4,3,2,1,0:T(8,128)(2,1)S(1)}, bf16[2,64,1,8,256]{4,3,2,1,0:T(8,128)(2,1)}, u32[]{:S(2)}) copy-start(bf16[2,64,1,8,256]{4,3,2,1,0:T(8,128)(2,1)} %copy-done.12) | copy-start | bytes 1572868
  412.1 81.9 %copy-start.15 = (f32[2,64,8,256]{3,2,1,0:T(8,128)S(1)}, f32[2,64,8,256]{3,2,1,0:T(8,128)}, u32[]{:S(2)}) copy-start(f32[2,64,8,256]{3,2,1,0:T(8,128)} %custom-call.2) | copy-start | bytes 3145732
  513.7 24.2 copy-start.16
  624.5 71.5 %copy-start.9 = (bf16[128,2048]{1,0:T(8,128)(2,1)S(1)}, bf16[128,2048]{1,0:T(8,128)(2,1)}, u32[]{:S(2)}) copy-start(bf16[128,2048]{1,0:T(8,128)(2,1)} %get-tuple-element.480) | copy-start | bytes 1572868
  624.5 1535.0 %reduce-scatter.9.cloned.1.call-start = ((), (), s32[]{:S(2)}) async-start(), calls=%async_computation.14 | async-start | bytes 71303168 | tf_op jit(solution)/shard_map/reduce_scatter | solution.py:331
  696.0 169.5 %copy-start.11 = (bf16[128,2048]{1,0:T(8,128)(2,1)S(1)}, bf16[128,2048]{1,0:T(8,128)(2,1)}, u32[]{:S(2)}) copy-start(bf16[128,2048]{1,0:T(8,128)(2,1)} %copy-done.10) | copy-start | bytes 1572868
  914.2 1885.5 %reduce-scatter.11.cloned.1.call-start = ((), (), s32[]{:S(2)}) async-start(), calls=%async_computation.15 | async-start | bytes 71303168 | tf_op jit(solution)/shard_map/reduce_scatter | solution.py:333
  940.6 40.2 %copy-start.42 = (u32[32]{0:T(128)S(1)}, u32[32]{0:T(128)}, u32[]{:S(2)}) copy-start(u32[32]{0:T(128)} %constant.106) | copy-start | bytes 388
  940.6 42.7 %copy-start.6 = (bf16[2,64,2048]{2,1,0:T(8,128)(2,1)S(1)}, bf16[2,64,2048]{2,1,0:T(8,128)(2,1)}, u32[]{:S(2)}) copy-start(bf16[2,64,2048]{2,1,0:T(8,128)(2,1)} %param.35) | copy-start | bytes 1572868
  940.6 42.7 %copy-start.29 = (f32[2,64]{1,0:T(2,128)S(1)}, f32[2,64]{1,0:T(2,128)}, u32[]{:S(2)}) copy-start(f32[2,64]{1,0:T(2,128)} %copy-done.28) | copy-start | bytes 1540
  940.6 2016.3 %all-reduce.12.cloned.1.call-start = ((), (), s32[]{:S(2)}) async-start(), calls=%async_computation.16 | async-start | bytes 12582912 | tf_op jit(solution)/shard_map/psum | solution.py:339
  2804.6 87.2 %copy-start.33 = (f32[128]{0:T(128)S(1)}, f32[128]{0:T(128)}, u32[]{:S(2)}) copy-start(f32[128]{0:T(128)} %copy-done.32) | copy-start | bytes 1540
  2890.2 76.4 %copy-start.43 = (f32[128]{0:T(128)}, f32[128]{0:T(128)S(1)}, u32[]{:S(2)}) copy-start(f32[128]{0:T(128)S(1)} %convert_element_type.290) | copy-start | bytes 1540
  (27 other events, 135.6 us)
Sparse Core Ops, SparseCore 0:
  9.6 131.5 all-gather.16
  143.3 75.1 all-gather.22
  221.2 73.1 all-gather.18
  297.0 73.1 all-gather.20
  372.2 73.1 all-gather.30
  448.1 77.3 all-gather.28
  527.1 168.8 all-gather.24
  697.6 167.8 all-gather.26
  869.6 178.5 reduce-scatter.6
  1052.3 466.8 reduce-scatter.4
  1523.4 636.0 reduce-scatter.8
  2163.6 636.0 reduce-scatter.10
  2803.7 153.2 all-reduce.11
where the time goes:
time: 2980 us; the launch traced here: 2970 us
  waiting for transfers between devices  2270 us (76%)
  blocking collectives  270 us (9%)
  matrix products  227 us (8%)
  local copies, waits for them, and re-layouts  133 us (4%)
  other arithmetic  51.3 us (2%)
    reduce_scatter x1, waiting for transfers between devices, local(): lax.psum_scatter(grad_w_up, 'wide', scatter_dimension=0, tiled=True)  637 us
    reduce_scatter x1, waiting for transfers between devices, local(): lax.psum_scatter(grad_w_down, 'wide', scatter_dimension=0, tiled=True)  636 us
    reduce_scatter x1, waiting for transfers between devices, local(): lax.psum_scatter(grad_w_qkv, 'wide', scatter_dimension=0, tiled=True)  469 us
    all_gather x1, waiting for transfers between devices, local(): lax.all_gather(w_down, 'wide', axis=0, tiled=True)  151 us
    unnamed x108, local copies, waits for them, and re-layouts  65.1 us
    all_gather x1, waiting for transfers between devices, local(): lax.all_gather(value_heads.reshape(seq_count, span_len, model_width), 'wi...  64.6 us
    unnamed x1, blocking collectives  59.8 us
  transfers between devices with their start and end apart: 13, of which 12 were waited for; matrix products, arithmetic and copies ran while one was open for 13% of the time, Pallas kernels for 0%

commit v1 on v0

v1 whole, which is shorter than its diff:
```python
import jax
import jax.numpy as jnp
from jax import lax
from jax.sharding import Mesh
from jax.sharding import PartitionSpec as P

HEADS = 8
HEAD_DIM = 256
ROT = 64

EPS = 1e-05
MASKED = -1e30
ROT_BASE = 10000.0
ROOT_HALF = 0.7071067811865476
INV_ROOT_TAU = 0.3989422804014327

WIDE = ("head", "sub")
f32 = jnp.float32
bf16 = jnp.bfloat16


def rotary_tables(places):
    halves = ROT // 2
    inverse = ROT_BASE ** (-2.0 * jnp.arange(halves, dtype=f32) / ROT)
    angles = places.astype(f32)[:, None] * inverse[None, :]
    return (jnp.cos(angles), jnp.sin(angles))


def rotate(rows, cosine, sine):
    halves = ROT // 2
    first = rows[..., :halves]
    second = rows[..., halves:ROT]
    return jnp.concatenate(
        [
            first * cosine - second * sine,
            second * cosine + first * sine,
            rows[..., ROT:],
        ],
        axis=-1,
    )


def norm_stats(values):
    average = jnp.mean(values, axis=-1, keepdims=True)
    centered = values - average
    variance = jnp.mean(centered * centered, axis=-1, keepdims=True)
    scale = lax.rsqrt(variance + EPS)
    return (centered * scale, scale)


def exchange(parts, count):
    me = lax.axis_index("sub")
    got = []
    for shift in range(count):
        part = parts(lax.rem(me + shift, count))
        if shift:
            part = lax.ppermute(part, "sub", [(j, (j + shift) % count) for j in range(count)])
        got.append(part)
    stacked = jnp.stack(got)
    order = lax.rem(me - jnp.arange(count, dtype=jnp.int32) + count, count)
    if count == 2:
        return jnp.where(me == 0, stacked, stacked[::-1])
    return jnp.take(stacked, order, axis=0)


def over_dp(low):
    count = lax.axis_size("dp")
    if count == 2:
        other = lax.ppermute(low, "dp", [(0, 1), (1, 0)])
        return low.astype(f32) + other.astype(f32)
    return lax.psum(low.astype(f32), "dp")


def dot(a, b, dims, out=f32):
    return lax.dot_general(a, b, (dims, ((), ())), preferred_element_type=f32).astype(out)


NN = ((1,), (0,))
NT = ((1,), (1,))
TN = ((0,), (0,))


def local(
    tokens,
    lengths,
    gain_one,
    shift_one,
    w_qkv,
    b_qkv,
    w_dense,
    b_dense,
    gain_two,
    shift_two,
    w_up,
    b_up,
    w_down,
    b_down,
    cotangent,
):
    S, span, D = tokens.shape
    M = lax.axis_size("sub")
    W = lax.axis_size("head") * M
    G = M // S
    L = span * W
    T = S * L
    R = w_qkv.shape[0]
    CW = D // W
    FW = w_down.shape[0]
    FF = w_up.shape[1]
    me = lax.axis_index(WIDE)
    sub = lax.axis_index("sub")
    own_seq = sub // G
    own_chunk = lax.rem(sub, G)
    Q = L // G

    small = jnp.concatenate([gain_one, shift_one, gain_two, shift_two, b_qkv, b_dense, b_down])
    small_all = lax.all_gather(small, WIDE)
    pieces = []
    start = 0
    for piece in (gain_one, shift_one, gain_two, shift_two, b_qkv, b_dense, b_down):
        pieces.append(small_all[:, start : start + piece.shape[0]].reshape(-1).astype(f32))
        start += piece.shape[0]
    g1, s1, g2, s2, bq_all, bd_all, bo_all = pieces
    bq = lax.dynamic_index_in_dim(bq_all.reshape(3, W, CW), me, 1, keepdims=False).reshape(3 * CW)

    x_all = lax.all_gather(tokens, WIDE)
    c_all = lax.all_gather(cotangent, WIDE)

    sent = jnp.concatenate(
        [
            w_qkv.reshape(R, 3, W, CW).transpose(2, 0, 1, 3).reshape(W, R, 3 * CW),
            w_up.reshape(R, W, FW).transpose(1, 0, 2),
        ],
        axis=-1,
    )
    cols = lax.all_to_all(sent, WIDE, 0, 0, tiled=True).reshape(D, 3 * CW + FW)
    wq, wu = cols[:, : 3 * CW], cols[:, 3 * CW :]
    wo = jnp.concatenate([w_down, w_dense], axis=0)

    place = (
        jnp.arange(W, dtype=jnp.int32)[:, None, None] * span
        + jnp.arange(span, dtype=jnp.int32)[None, None, :]
    )
    valid = (place < lengths[None, :, None]).reshape(T, 1)
    go = jnp.where(valid, c_all.reshape(T, D), jnp.zeros((), bf16))

    n_all, _ = norm_stats(x_all.reshape(T, D).astype(f32))
    h1 = (n_all * g1 + s1).astype(bf16)
    h2 = (n_all * g2 + s2).astype(bf16)

    joined = dot(h1, wq, NN) + bq
    cosine, sine = rotary_tables(jnp.arange(L, dtype=jnp.int32))
    early = CW >= ROT
    joined = joined.reshape(W, S, span, 3, CW)
    if early:
        here = sub == 0 if HEAD_DIM // CW > 1 else True
        cos_w = jnp.where(here, cosine, 1.0).reshape(W, 1, span, 1, ROT // 2)
        sin_w = jnp.where(here, sine, 0.0).reshape(W, 1, span, 1, ROT // 2)
        joined = jnp.concatenate(
            [rotate(joined[..., :2, :], cos_w, sin_w), joined[..., 2:, :]], axis=3
        ).astype(bf16)

    def columns_of(i):
        return lax.dynamic_index_in_dim(joined, i // G, 1, keepdims=False).reshape(L, 3, CW)

    heads = exchange(columns_of, M).transpose(2, 1, 0, 3).reshape(3, L, M * CW)
    if not early:
        heads = jnp.stack(
            [rotate(heads[0], cosine, sine), rotate(heads[1], cosine, sine), heads[2]]
        ).astype(bf16)
    queries = lax.dynamic_slice_in_dim(heads[0], own_chunk * Q, Q, 0)
    keys, values = heads[1], heads[2]

    length = lax.dynamic_index_in_dim(lengths, own_seq, 0, keepdims=False)
    q_places = own_chunk * Q + jnp.arange(Q, dtype=jnp.int32)
    k_places = jnp.arange(L, dtype=jnp.int32)
    allowed = (k_places[None, :] <= q_places[:, None]) & (k_places[None, :] < length)
    score_scale = HEAD_DIM ** (-0.5)
    scores = jnp.where(allowed, dot(queries, keys, NT) * score_scale, MASKED)
    raised = jnp.exp(scores - jnp.max(scores, axis=-1, keepdims=True))
    soft = raised / jnp.sum(raised, axis=-1, keepdims=True)
    soft_low = soft.astype(bf16)
    attended = dot(soft_low, values, NN, bf16)

    def attended_of(i):
        return lax.dynamic_slice_in_dim(attended, i * CW, CW, 1)

    att = exchange(attended_of, M).reshape(S, W, span, CW).transpose(1, 0, 2, 3).reshape(T, CW)

    upper = dot(h2, wu, NN) + b_up.astype(f32)
    cdf = 0.5 * (1.0 + lax.erf(upper * ROOT_HALF))
    act = (upper * cdf).astype(bf16)
    slope = cdf + upper * jnp.exp(-0.5 * upper * upper) * INV_ROOT_TAU

    both = jnp.concatenate([act, att], axis=1)
    mixed_part = dot(both, wo, NN, bf16).reshape(W, S * span, D)
    mixed_own = lax.psum_scatter(mixed_part, WIDE, scatter_dimension=0, tiled=True).reshape(
        S, span, D
    )
    own_place = me * span + jnp.arange(span, dtype=jnp.int32)
    own_valid = (own_place[None, :] < lengths[:, None])[:, :, None]
    x_own = tokens.astype(f32)
    mixed = jnp.where(own_valid, x_own + mixed_own.astype(f32) + (bd_all + bo_all), 0.0).astype(bf16)

    grad_both = dot(go, wo, NT)
    gu = (grad_both[:, :FW] * slope).astype(bf16)
    ga = grad_both[:, FW:].astype(bf16).reshape(W, S, span, CW)

    def grads_of(i):
        part = lax.dynamic_index_in_dim(ga, i // G, 1, keepdims=False).reshape(L, CW)
        return lax.dynamic_slice_in_dim(part, lax.rem(i, G) * Q, Q, 0)

    g_att = exchange(grads_of, M).transpose(1, 0, 2).reshape(Q, M * CW)
    g_soft = dot(g_att, values, NT)
    delta = jnp.sum(soft * g_soft, axis=-1, keepdims=True)
    g_scores = (soft * (g_soft - delta)).astype(bf16)
    g_q = dot(g_scores, keys, NN) * score_scale
    g_k = dot(g_scores, queries, TN) * score_scale
    g_v = dot(soft_low, g_att, TN)
    if G > 1:
        g_q = lax.dynamic_update_slice_in_dim(
            jnp.zeros((L, M * CW), f32), g_q, own_chunk * Q, 0
        )
    g_joined = jnp.stack(
        [rotate(g_q, cosine, -sine), rotate(g_k, cosine, -sine), g_v], axis=1
    ).astype(bf16)

    def joined_of(i):
        return lax.dynamic_slice_in_dim(g_joined, i * CW, CW, 2)

    gj = exchange(joined_of, M).reshape(S, G, L, 3, CW)
    gj = gj[:, 0] if G == 1 else jnp.sum(gj.astype(f32), axis=1).astype(bf16)
    gj = gj.reshape(S, W, span, 3 * CW).transpose(1, 0, 2, 3).reshape(T, 3 * CW)

    back = jnp.concatenate([gj, gu], axis=1)
    w_back = jnp.concatenate(
        [(wq.astype(f32) * g1[:, None]).astype(bf16), (wu.astype(f32) * g2[:, None]).astype(bf16)],
        axis=1,
    )
    f_part = dot(back, w_back, NT, bf16).reshape(W, S * span, D)
    f_own = (
        lax.psum_scatter(f_part, WIDE, scatter_dimension=0, tiled=True)
        .reshape(S, span, D)
        .astype(f32)
    )
    n_own, r_own = norm_stats(x_own)
    grad_x = r_own * (
        f_own
        - jnp.mean(f_own, axis=-1, keepdims=True)
        - n_own * jnp.mean(f_own * n_own, axis=-1, keepdims=True)
    )
    go_own = jnp.where(own_valid, cotangent.astype(f32), 0.0)
    token_grad = (go_own + grad_x).astype(bf16)

    gw_out = dot(both, go, TN, bf16)
    gw_out = over_dp(gw_out)
    go_cols = lax.dynamic_slice_in_dim(go, me * CW, CW, 1)
    gb_out = jnp.sum(go_cols.astype(f32), axis=0)
    gb_up = jnp.sum(gu.astype(f32), axis=0)
    gb_q = jnp.sum(gj.astype(f32), axis=0)
    tail = 8

    def to_rows(grad, bias):
        width = grad.shape[1]
        block = jnp.concatenate(
            [
                grad.reshape(W, R, width),
                jnp.broadcast_to(bias.astype(bf16)[None, None, :], (W, tail, width)),
            ],
            axis=1,
        )
        got = over_dp(lax.all_to_all(block, WIDE, 0, 0, tiled=True))
        return (got[:, :R].transpose(1, 0, 2), got[:, R])

    gw_up, gb_up_all = to_rows(dot(h2, gu, TN, bf16), gb_up)
    gw_q, gb_q_all = to_rows(dot(h1, gj, TN, bf16), gb_q)
    gw_up = gw_up.reshape(R, FF)
    gw_q = gw_q.reshape(R, W, 3, CW).transpose(0, 2, 1, 3).reshape(R, 3 * D)
    gb_up_all = gb_up_all.reshape(FF)
    gb_q_all = gb_q_all.reshape(W, 3, CW).transpose(1, 0, 2).reshape(3 * D)

    def norm_grads(gw, gb, w, gain, shift):
        wf = w.astype(f32)
        shift_grad = jnp.sum(wf * gb[None, :], axis=1)
        gain_grad = (jnp.sum(wf * gw, axis=1) - shift.astype(f32) * shift_grad) / gain.astype(f32)
        return (gain_grad, shift_grad)

    gg1, gs1 = norm_grads(gw_q, gb_q_all, w_qkv, gain_one, shift_one)
    gg2, gs2 = norm_grads(gw_up, gb_up_all, w_up, gain_two, shift_two)
    gb_q_own = lax.dynamic_slice_in_dim(gb_q_all, me * 3 * CW, 3 * CW, 0)
    vectors = over_dp(jnp.concatenate([gb_out, gb_up]).astype(bf16))
    gb_out, gb_up = vectors[:CW], vectors[CW:]
    return (
        mixed,
        token_grad,
        gg1,
        gs1,
        gw_q,
        gb_q_own,
        gw_out[FW:],
        gb_out,
        gg2,
        gs2,
        gw_up,
        gb_up,
        gw_out[:FW],
        gb_out,
    )


def solution(mesh):
    dp, wide = mesh.shape["dp"], mesh.shape["wide"]
    split = Mesh(mesh.devices.reshape(dp, HEADS, wide // HEADS), ("dp",) + WIDE)
    rows = P("dp", WIDE, None)
    mat, vec = P(WIDE, None), P(WIDE)
    in_specs = (rows, P("dp"), vec, vec, mat, vec, mat, vec, vec, vec, mat, vec, mat, vec, rows)
    out_specs = (rows, rows, vec, vec, mat, vec, mat, vec, vec, vec, mat, vec, mat, vec)
    return jax.shard_map(local, mesh=split, in_specs=in_specs, out_specs=out_specs, check_vma=False)
```

time: 2980 us -> 603 us (0.20)
  waiting for transfers between devices: 2270 us -> 193 us
  blocking collectives: 270 us -> 111 us
  matrix products: 227 us -> 88 us
  local copies, waits for them, and re-layouts: 133 us -> 70.3 us
  other arithmetic: 51.3 us -> 91.5 us
    reduce_scatter x4 -> x2, waiting for transfers between devices: 1790 us -> 3.38 us  [the longest x1 3.38 us: local(): lax.psum_scatter(mixed_part, WIDE, scatter_dimension=0, tiled=True)]
    all_gather x8 -> x2, waiting for transfers between devices: 441 us -> 26.3 us  [the longest x1 26.3 us: local(): c_all = lax.all_gather(cotangent, WIDE)]
    dot_general x28 -> x14, matrix products: 227 us -> 88 us  [dot(): lax.dot_general(a, b, (dims, ((), ())), preferred_element_type=f32)]
    all_gather x10 -> x1, blocking collectives: 205 us -> 111 us  [local(): small_all = lax.all_gather(small, WIDE)]
    all_to_all x0 -> x3, waiting for transfers between devices: none -> 93.7 us  [the longest x2 93.7 us: to_rows(): got = over_dp(lax.all_to_all(block, WIDE, 0, 0, tiled=True))]
    ppermute x0 -> x8, waiting for transfers between devices: none -> 68.3 us  [the longest x4 68 us: over_dp(): other = lax.ppermute(low, 'dp', [(0, 1), (1, 0)])]
    unnamed x1 -> x0, blocking collectives: 59.8 us -> none
    dynamic_slice x20 -> x5, local copies, waits for them, and re-layouts: 51.1 us -> 2.16 us  [the longest x1 0.85 us: columns_of(): lax.dynamic_index_in_dim(joined, i // G, 1, keepdims=False)]
  transfers between devices with their start and end apart: 13 -> 15, of which waited for: 12 -> 7; matrix products, arithmetic and copies ran while one was open for 13% -> 31% of each run, Pallas kernels for 0% -> 0%
where the time goes in v1:
time: 603 us; the launch traced here: 598 us
  waiting for transfers between devices  193 us (32%)
  blocking collectives  111 us (18%)
  other arithmetic  91.5 us (15%)
  matrix products  88 us (15%)
  local copies, waits for them, and re-layouts  70.3 us (12%)
  starting transfers between devices  29.8 us (5%)
  between operations  14.9 us (2%)
    all_gather x1, blocking collectives, local(): small_all = lax.all_gather(small, WIDE)  111 us
    all_to_all x2, waiting for transfers between devices, to_rows(): got = over_dp(lax.all_to_all(block, WIDE, 0, 0, tiled=True))  93.7 us
    dot_general x14, matrix products, dot(): lax.dot_general(a, b, (dims, ((), ())), preferred_element_type=f32)  88 us
    ppermute x4, waiting for transfers between devices, over_dp(): other = lax.ppermute(low, 'dp', [(0, 1), (1, 0)])  68 us
    unnamed x97, local copies, waits for them, and re-layouts  26.9 us
    all_gather x1, waiting for transfers between devices, local(): c_all = lax.all_gather(cotangent, WIDE)  26.3 us
    all_to_all x2, starting transfers between devices, to_rows(): got = over_dp(lax.all_to_all(block, WIDE, 0, 0, tiled=True))  15.4 us
  transfers between devices with their start and end apart: 15, of which 7 were waited for; matrix products, arithmetic and copies ran while one was open for 31% of the time, Pallas kernels for 0%

profile of v1, /device:TPU:0, one launch (start us, length us, event | category | flops | bytes accessed | tf_op | source)
XLA Modules:
  0.0 598.5 jit_solution(7104299305086594180)
XLA Ops:
  8.7 4.1 copy.144
  18.0 7.6 %all-to-all-start = ((bf16[16,128,896]{1,2,0:T(8,128)(2,1)}), bf16[16,128,896]{1,2,0:T(8,128)(2,1)}, u32[]{:S(2)}, u32[]{:S(2)}) async-start(bf16[16,128,896]{1,2,0:T(8,128)(2,1)} %pad_maximum_fusion), calls=%async_computation | async-start | bytes 7340032 | tf_op jit(solution)/shard_map/all_to_all | solution.py:136
  27.3 110.9 %all-gather.3 = bf16[16,1,1152]{2,1,0:T(2,128)(2,1)S(1)} all-gather(bf16[1,1,1152]{2,1,0:T(2,128)(2,1)S(1)} %reshape.437), channel_id=3, replica_groups=mesh['dp'=2,'head'=8,'sub'=2] {'head','sub'}, dimensions={0}, use_global_device_ids=true | all-gather | bytes 39168 | tf_op jit(solution)/shard_map/all_gather | solution.py:117
  139.6 3.2 constant_dynamic-update-slice_fusion.2
  146.6 6.1 %copy.145 = bf16[16,128,896]{2,1,0:T(8,128)(2,1)} copy(bf16[16,128,896]{1,2,0:T(8,128)(2,1)} %all-to-all-done) | data formatting | bytes 7340032 | tf_op jit(solution)/shard_map/all_to_all | solution.py:136
  152.7 3.3 multiply_convert_fusion
  156.1 5.0 convert_reduce_fusion
  161.1 11.5 %multiply_reduce_fusion = (f32[16,2,64]{2,1,0:T(2,128)S(1)}, f32[16,2,64,2048]{3,2,1,0:T(8,128)}) fusion(f32[16,2,64]{2,1,0:T(2,128)S(1)} %bitcast.189, bf16[16,2,64,2048]{3,2,1,0:T(8,128)(2,1)} %bitcast.152), kind=kLoop, calls=%fused_computation.5 | loop fusion | flops 16775168 | bytes 25182208 | tf_op jit(solution)/shard_map/reduce_sum | solution.py:46
  172.8 9.6 %add_convert_fusion.2 = (bf16[2048,2048]{1,0:T(8,128)(2,1)}, bf16[2048,2048]{1,0:T(8,128)(2,1)S(1)}) fusion(bf16[32,64,2048]{2,1,0:T(8,128)(2,1)} %all-gather.7.cloned.1.call-done, f32[2048]{0:T(1024)S(1)} %get-tuple-element.108, f32[2048]{0:T(1024)S(1)} %get-tuple-element.105, f32[2048]{0:T(1024)S(1)} %rsqrt.21, f32[2048]{0:T(1024)S(1)} %div.67, ...), kind=kLoop, calls=%fused_computation.4 | loop fusion | flops 37748736 | bytes 25214976 | tf_op jit(solution)/shard_map/convert_element_type | solution.py:149
  182.4 6.4 %convolution_add_fusion = f32[2048,384]{1,0:T(8,128)S(1)} fusion(bf16[2048,2048]{1,0:T(8,128)(2,1)S(1)} %get-tuple-element.85, f32[384]{0:T(512)S(1)} %bitcast.199, bf16[2048,896]{1,0:T(8,128)(2,1)} %bitcast.157), kind=kOutput, calls=%fused_computation.54 | convolution fusion | flops 3222011904 | bytes 13108736 | tf_op jit(solution)/shard_map/dot_general | solution.py:75
  191.9 3.1 convert.61
  197.5 26.3 %all-gather.9.cloned.1.call-done = bf16[32,64,2048]{2,1,0:T(8,128)(2,1)} async-done(((bf16[2,64,2048]{2,1,0:T(8,128)(2,1)}), bf16[32,64,2048]{2,1,0:T(8,128)(2,1)}) %all-gather.9.cloned.1.call-update) | async-done | bytes 8388624 | tf_op jit(solution)/shard_map/all_gather | solution.py:127
  223.8 7.4 %bitcast_select_fusion = bf16[2048,2048]{1,0:T(8,128)(2,1)} fusion(bf16[32,64,2048]{2,1,0:T(8,128)(2,1)} %all-gather.9.cloned.1.call-done, pred[2048]{0:T(1024)(128)(4,1)S(1)} %lt.97), kind=kLoop, calls=%fused_computation.7 | loop fusion | flops 4194304 | bytes 16779264 | tf_op jit(solution)/shard_map/jit(_where)/select_n | solution.py:145
  231.2 10.1 %fusion.82 = f32[2048,640]{1,0:T(8,128)S(1)} fusion(bf16[2048,2048]{1,0:T(8,128)(2,1)} %bitcast_select_fusion, bf16[640,2048]{1,0:T(8,128)(2,1)} %constant_dynamic-update-slice_fusion.1), kind=kOutput, calls=%fused_computation.185 | convolution fusion | flops 5368709120 | bytes 16252928 | tf_op jit(solution)/shard_map/dot_general | solution.py:75
  244.7 6.2 %pad_maximum_fusion.3 = bf16[16,2,64,3,128]{4,3,2,1,0:T(4,128)(2,1)S(1)} fusion(bf16[16,2,64,1,128]{4,3,2,1,0:T(2,128)(2,1)S(1)} %slice.150, bf16[16,2,64,2,64]{4,3,2,1,0:T(2,128)(2,1)S(1)} %slice.149, bf16[16,2,64,2,32]{4,3,2,1,0:T(2,128)(2,1)S(1)} %get-tuple-element.87, bf16[16,2,64,2,32]{4,3,2,1,0:T(2,128)(2,1)S(1)} %get-tuple-element.86), kind=kLoop, calls=%fused_computation.60 | loop fusion | flops 6291456 | bytes 3145728 | tf_op jit(solution)/shard_map/concatenate | solution.py:159
  255.6 4.6 slice.163
  260.3 5.3 copy.180
  281.7 8.6 %fusion.77 = (bf16[512]{0:T(512)(128)(2,1)S(1)}, bf16[2048,512]{0,1:T(8,128)(2,1)}, f32[2048,512]{0,1:T(8,128)}) fusion(f32[2048,512]{0,1:T(8,128)S(1)} %copy-done.13, f32[512]{0:T(512)S(1)} %convert_element_type.257, bf16[2048,2048]{1,0:T(8,128)(2,1)S(1)} %bitcast.164, bf16[2048,896]{1,0:T(8,128)(2,1)S(1)} %bitcast.159), kind=kOutput, calls=%fused_computation.182 | convolution fusion | flops 4307549696 | bytes 20974592 | tf_op jit(solution)/shard_map/dot_general | solution.py:75
  300.9 13.9 %convolution_convert_fusion = bf16[2048,2048]{1,0:T(8,128)(2,1)} fusion(bf16[2048,512]{0,1:T(8,128)(2,1)} %get-tuple-element.75, bf16[2048,384]{0,1:T(8,128)(2,1)} %copy.161, bf16[2048,512]{1,0:T(8,128)(2,1)} %multiply_convert_fusion, bf16[2048,384]{1,0:T(8,128)(2,1)} %multiply_convert_fusion.3), kind=kOutput, calls=%fused_computation.9 | convolution fusion | flops 7535067136 | bytes 15728640 | tf_op jit(solution)/shard_map/dot_general | solution.py:75
  320.4 11.1 %convolution_convert_fusion.1 = bf16[2048,2048]{1,0:T(8,128)(2,1)} fusion(bf16[640,2048]{1,0:T(8,128)(2,1)} %constant_dynamic-update-slice_fusion.1, bf16[2048,128]{0,1:T(8,128)(2,1)S(1)} %copy.153, bf16[2048,512]{0,1:T(8,128)(2,1)S(1)} %multiply_convert_fusion.2), kind=kOutput, calls=%fused_computation.10 | convolution fusion | flops 5378146304 | bytes 13631488 | tf_op jit(solution)/shard_map/dot_general | solution.py:75
  333.1 11.7 %bitcast_convert_fusion = bf16[2048,384]{1,0:T(8,128)(2,1)S(1)} fusion(f32[16,2,64,2048]{3,2,1,0:T(8,128)} %get-tuple-element.83, f32[2048]{0:T(1024)S(1)} %get-tuple-element.106, f32[2048]{0:T(1024)S(1)} %get-tuple-element.107, f32[16,2,64]{2,1,0:T(2,128)S(1)} %add_rsqrt_fusion, f32[16,2,64]{2,1,0:T(2,128)S(1)} %bitcast.190, ...), kind=kOutput, calls=%fused_computation.51 | convolution fusion | flops 3242983424 | bytes 19955712 | tf_op jit(solution)/shard_map/dot_general | solution.py:75
  346.2 3.7 all-to-all-start.1
  349.9 8.6 %convolution_convert_fusion.3 = bf16[2048,512]{1,0:T(8,128)(2,1)S(1)} fusion(bf16[2048,2048]{1,0:T(8,128)(2,1)} %get-tuple-element.84, bf16[2048,512]{0,1:T(8,128)(2,1)} %get-tuple-element.75), kind=kOutput, calls=%fused_computation.53 | convolution fusion | flops 4296015872 | bytes 12582912 | tf_op jit(solution)/shard_map/dot_general | solution.py:75
  360.1 49.6 %all-to-all-done.1 = bf16[16,136,384]{2,1,0:T(8,128)(2,1)S(1)} async-done(((bf16[16,136,384]{2,1,0:T(8,128)(2,1)}), bf16[16,136,384]{2,1,0:T(8,128)(2,1)S(1)}, u32[]{:S(2)}, u32[]{:S(2)}) %all-to-all-start.1) | async-done | bytes 1671200 | tf_op jit(solution)/shard_map/all_to_all | solution.py:272
  409.8 11.6 %all-to-all-start.2 = ((bf16[16,136,512]{2,1,0:T(8,128)(2,1)}), bf16[16,136,512]{2,1,0:T(8,128)(2,1)}, u32[]{:S(2)}, u32[]{:S(2)}) async-start(bf16[16,136,512]{2,1,0:T(8,128)(2,1)} %pad_maximum_fusion.2), calls=%async_computation.4 | async-start | bytes 4456448 | tf_op jit(solution)/shard_map/all_to_all | solution.py:272
  421.4 9.8 %convolution_convert_fusion.2 = bf16[640,2048]{1,0:T(8,128)(2,1)} fusion(bf16[2048,2048]{1,0:T(8,128)(2,1)} %bitcast_select_fusion, bf16[2048,128]{0,1:T(8,128)(2,1)S(1)} %copy.153, bf16[2048,512]{0,1:T(8,128)(2,1)} %copy-done.18), kind=kOutput, calls=%fused_computation.47 | convolution fusion | flops 5375262720 | bytes 13631488 | tf_op jit(solution)/shard_map/dot_general | solution.py:75
  437.6 44.1 %all-to-all-done.2 = bf16[16,136,512]{2,1,0:T(8,128)(2,1)} async-done(((bf16[16,136,512]{2,1,0:T(8,128)(2,1)}), bf16[16,136,512]{2,1,0:T(8,128)(2,1)}, u32[]{:S(2)}, u32[]{:S(2)}) %all-to-all-start.2) | async-done | bytes 2228256 | tf_op jit(solution)/shard_map/all_to_all | solution.py:272
  483.3 43.7 %collective-permute-done.6 = bf16[640]{0:T(1024)(128)(2,1)S(1)} collective-permute-done((bf16[640]{0:T(1024)(128)(2,1)S(1)}, bf16[640]{0:T(1024)(128)(2,1)S(1)}, u32[]{:S(2)}, u32[]{:S(2)}) %collective-permute-start.6) | collective-permute-done | bytes 1312 | tf_op jit(solution)/shard_map/ppermute | solution.py:69
  527.6 3.6 convert_add_fusion
  538.7 3.6 copy.164
  550.1 24.3 %collective-permute-done.7 = bf16[16,136,512]{2,1,0:T(8,128)(2,1)} collective-permute-done((bf16[16,136,512]{2,1,0:T(8,128)(2,1)}, bf16[16,136,512]{2,1,0:T(8,128)(2,1)}, u32[]{:S(2)}, u32[]{:S(2)}) %collective-permute-start.7) | collective-permute-done | bytes 2228256 | tf_op jit(solution)/shard_map/ppermute | solution.py:69
  585.1 3.4 reduce-scatter.3.cloned.1.call-done
  (224 shorter events, 101.4 us)
Async XLA Ops:
  7.2 148.9 %all-gather.7.cloned.1.call-start = ((), (), s32[]{:S(2)}) async-start(), calls=%async_computation.7 | async-start | bytes 8912896 | tf_op jit(solution)/shard_map/all_gather | solution.py:126
  7.9 215.9 %all-gather.9.cloned.1.call-start = ((), (), s32[]{:S(2)}) async-start(), calls=%async_computation.8 | async-start | bytes 8912896 | tf_op jit(solution)/shard_map/all_gather | solution.py:127
  17.9 8.5 %copy-start.26 = (bf16[128]{0:T(256)(128)(2,1)S(1)}, bf16[128]{0:T(256)(128)(2,1)}, u32[]{:S(2)}) copy-start(bf16[128]{0:T(256)(128)(2,1)} %param.23) | copy-start | bytes 772
  18.0 8.7 %copy-start.28 = (bf16[128]{0:T(256)(128)(2,1)S(1)}, bf16[128]{0:T(256)(128)(2,1)}, u32[]{:S(2)}) copy-start(bf16[128]{0:T(256)(128)(2,1)} %param.24) | copy-start | bytes 772
  18.0 8.9 %copy-start.33 = (bf16[384]{0:T(512)(128)(2,1)S(1)}, bf16[384]{0:T(512)(128)(2,1)}, u32[]{:S(2)}) copy-start(bf16[384]{0:T(512)(128)(2,1)} %param.20) | copy-start | bytes 2308
  18.0 9.1 %copy-start.34 = (bf16[128]{0:T(256)(128)(2,1)S(1)}, bf16[128]{0:T(256)(128)(2,1)}, u32[]{:S(2)}) copy-start(bf16[128]{0:T(256)(128)(2,1)} %param.22) | copy-start | bytes 772
  18.0 9.3 %copy-start.37 = (bf16[128]{0:T(256)(128)(2,1)S(1)}, bf16[128]{0:T(256)(128)(2,1)}, u32[]{:S(2)}) copy-start(bf16[128]{0:T(256)(128)(2,1)} %param.28) | copy-start | bytes 772
  18.0 128.6 %all-to-all-start = ((bf16[16,128,896]{1,2,0:T(8,128)(2,1)}), bf16[16,128,896]{1,2,0:T(8,128)(2,1)}, u32[]{:S(2)}, u32[]{:S(2)}) async-start(bf16[16,128,896]{1,2,0:T(8,128)(2,1)} %pad_maximum_fusion), calls=%async_computation | async-start | bytes 7340032 | tf_op jit(solution)/shard_map/all_to_all | solution.py:136
  25.6 117.2 %copy-start.20 = (bf16[128,2048]{1,0:T(8,128)(2,1)S(1)}, bf16[128,2048]{1,0:T(8,128)(2,1)}, u32[]{:S(2)}) copy-start(bf16[128,2048]{1,0:T(8,128)(2,1)} %param.21) | copy-start | bytes 1572868
  25.6 556.8 %reduce-scatter.5.cloned.1.call-start = ((), (), s32[]{:S(2)}) async-start(), calls=%async_computation.6 | async-start | bytes 8912896 | tf_op jit(solution)/shard_map/reduce_scatter | solution.py:242
  138.2 14.5 %copy-start.21 = (bf16[16,1,1152]{2,0,1:T(8,128)(2,1)}, bf16[16,1,1152]{2,0,1:T(8,128)(2,1)S(1)}, u32[]{:S(2)}) copy-start(bf16[16,1,1152]{2,0,1:T(8,128)(2,1)S(1)} %copy.185) | copy-start | bytes 110596
  231.2 10.5 %copy-start.1 = (f32[16,2,64,3,128]{4,3,2,1,0:T(4,128)S(1)}, f32[16,2,64,3,128]{4,3,2,1,0:T(4,128)}, u32[]{:S(2)}) copy-start(f32[16,2,64,3,128]{4,3,2,1,0:T(4,128)} %reshape.400) | copy-start | bytes 9437188
  231.2 10.5 %copy-start.15 = (f32[16,64,32]{2,1,0:T(8,128)S(1)}, f32[16,64,32]{2,1,0:T(8,128)}, u32[]{:S(2)}) copy-start(f32[16,64,32]{2,1,0:T(8,128)} %get-tuple-element.109) | copy-start | bytes 393220
  231.2 10.5 %copy-start.16 = (f32[16,64,32]{2,1,0:T(8,128)S(1)}, f32[16,64,32]{2,1,0:T(8,128)}, u32[]{:S(2)}) copy-start(f32[16,64,32]{2,1,0:T(8,128)} %get-tuple-element.110) | copy-start | bytes 393220
  241.4 24.8 %collective-permute-start.2 = (bf16[1024,128]{1,0:T(8,128)(2,1)S(1)}, bf16[1024,128]{1,0:T(8,128)(2,1)}, u32[]{:S(2)}, u32[]{:S(2)}) collective-permute-start(bf16[1024,128]{1,0:T(8,128)(2,1)S(1)} %bitcast.187), channel_id=1, source_target_pairs={{0,1},{1,0},{2,3},{3,2},{4,5},{5,4},{6,7},{7,6},{8,9},{9,8},{10,11... | collective-permute-start | bytes 786440 | tf_op jit(solution)/shard_map/ppermute | solution.py:57
  252.4 15.2 %collective-permute-start = (bf16[1024,3,128]{0,2,1:T(8,128)(2,1)S(1)}, bf16[1024,3,128]{0,2,1:T(8,128)(2,1)}, u32[]{:S(2)}, u32[]{:S(2)}) collective-permute-start(bf16[1024,3,128]{0,2,1:T(8,128)(2,1)S(1)} %copy.148), channel_id=1, source_target_pairs={{0,1},{1,0},{2,3},{3,2},{4,5},{5,4},{6,7},{7,6},{8,9},{9,8},{10,11... | collective-permute-start | bytes 2359304 | tf_op jit(solution)/shard_map/ppermute | solution.py:57
  278.7 11.6 %collective-permute-start.3 = (bf16[1024,3,128]{0,2,1:T(8,128)(2,1)S(1)}, bf16[1024,3,128]{0,2,1:T(8,128)(2,1)S(1)}, u32[]{:S(2)}, u32[]{:S(2)}) collective-permute-start(bf16[1024,3,128]{0,2,1:T(8,128)(2,1)S(1)} %get-tuple-element.91), channel_id=1, source_target_pairs={{0,1},{1,0},{2,3},{3,2},{4,5},{5,4},{6,7},{7,6},{8,9},{9,8},{10,11... | collective-permute-start | bytes 2359304 | tf_op jit(solution)/shard_map/ppermute | solution.py:57
  314.8 273.7 %reduce-scatter.3.cloned.1.call-start = ((), (), s32[]{:S(2)}) async-start(), calls=%async_computation.5 | async-start | bytes 8912896 | tf_op jit(solution)/shard_map/reduce_scatter | solution.py:197
  318.0 2.0 collective-permute-start.1
  319.7 11.9 %copy-start.18 = (bf16[2048,512]{0,1:T(8,128)(2,1)}, bf16[2048,512]{0,1:T(8,128)(2,1)S(1)}, u32[]{:S(2)}) copy-start(bf16[2048,512]{0,1:T(8,128)(2,1)S(1)} %multiply_convert_fusion.2) | copy-start | bytes 6291460
  346.2 63.6 %all-to-all-start.1 = ((bf16[16,136,384]{2,1,0:T(8,128)(2,1)}), bf16[16,136,384]{2,1,0:T(8,128)(2,1)S(1)}, u32[]{:S(2)}, u32[]{:S(2)}) async-start(bf16[16,136,384]{2,1,0:T(8,128)(2,1)} %pad_maximum_fusion.6), calls=%async_computation.3 | async-start | bytes 3342336 | tf_op jit(solution)/shard_map/all_to_all | solution.py:272
  409.8 23.5 %copy-start.9 = (bf16[16,136,384]{2,1,0:T(8,128)(2,1)}, bf16[16,136,384]{2,1,0:T(8,128)(2,1)S(1)}, u32[]{:S(2)}) copy-start(bf16[16,136,384]{2,1,0:T(8,128)(2,1)S(1)} %all-to-all-done.1) | copy-start | bytes 5013508
  409.8 71.9 %all-to-all-start.2 = ((bf16[16,136,512]{2,1,0:T(8,128)(2,1)}), bf16[16,136,512]{2,1,0:T(8,128)(2,1)}, u32[]{:S(2)}, u32[]{:S(2)}) async-start(bf16[16,136,512]{2,1,0:T(8,128)(2,1)} %pad_maximum_fusion.2), calls=%async_computation.4 | async-start | bytes 4456448 | tf_op jit(solution)/shard_map/all_to_all | solution.py:272
  421.4 11.4 %copy-start.5 = (bf16[2,64,2048]{2,1,0:T(8,128)(2,1)S(1)}, bf16[2,64,2048]{2,1,0:T(8,128)(2,1)}, u32[]{:S(2)}) copy-start(bf16[2,64,2048]{2,1,0:T(8,128)(2,1)} %param.15) | copy-start | bytes 1572868
  421.4 16.1 %copy-start.36 = (s32[2]{0:T(128)S(1)}, s32[2]{0:T(128)}, u32[]{:S(2)}) copy-start(s32[2]{0:T(128)} %param.16) | copy-start | bytes 28
  431.2 96.4 %collective-permute-start.5 = (bf16[640,2048]{1,0:T(8,128)(2,1)}, bf16[640,2048]{1,0:T(8,128)(2,1)}, u32[]{:S(2)}, u32[]{:S(2)}) collective-permute-start(bf16[640,2048]{1,0:T(8,128)(2,1)} %convolution_convert_fusion.2), channel_id=1, source_target_pairs={{0,16},{16,0},{1,17},{17,1},{2,18},{18,2},{3,19},{19,3},{4,20},{20... | collective-permute-start | bytes 7864328 | tf_op jit(solution)/shard_map/ppermute | solution.py:69
  433.3 101.5 %collective-permute-start.4 = (bf16[16,136,384]{2,1,0:T(8,128)(2,1)S(1)}, bf16[16,136,384]{2,1,0:T(8,128)(2,1)}, u32[]{:S(2)}, u32[]{:S(2)}) collective-permute-start(bf16[16,136,384]{2,1,0:T(8,128)(2,1)S(1)} %all-to-all-done.1), channel_id=1, source_target_pairs={{0,16},{16,0},{1,17},{17,1},{2,18},{18,2},{3,19},{19,3},{4,20},{20... | collective-permute-start | bytes 5013512 | tf_op jit(solution)/shard_map/ppermute | solution.py:69
  435.8 91.2 %collective-permute-start.6 = (bf16[640]{0:T(1024)(128)(2,1)S(1)}, bf16[640]{0:T(1024)(128)(2,1)S(1)}, u32[]{:S(2)}, u32[]{:S(2)}) collective-permute-start(bf16[640]{0:T(1024)(128)(2,1)S(1)} %pad_maximum_fusion.12), channel_id=1, source_target_pairs={{0,16},{16,0},{1,17},{17,1},{2,18},{18,2},{3,19},{19,3},{4,20},{20... | collective-permute-start | bytes 3848 | tf_op jit(solution)/shard_map/ppermute | solution.py:69
  481.7 92.7 %collective-permute-start.7 = (bf16[16,136,512]{2,1,0:T(8,128)(2,1)}, bf16[16,136,512]{2,1,0:T(8,128)(2,1)}, u32[]{:S(2)}, u32[]{:S(2)}) collective-permute-start(bf16[16,136,512]{2,1,0:T(8,128)(2,1)} %all-to-all-done.2), channel_id=1, source_target_pairs={{0,16},{16,0},{1,17},{17,1},{2,18},{18,2},{3,19},{19,3},{4,20},{20... | collective-permute-start | bytes 6684680 | tf_op jit(solution)/shard_map/ppermute | solution.py:69
  527.0 64.2 %copy-start.38 = (f32[128]{0:T(128)}, f32[128]{0:T(128)S(1)}, u32[]{:S(2)}) copy-start(f32[128]{0:T(128)S(1)} %slice.135) | copy-start | bytes 1540
  549.5 27.9 %copy-start.30 = (f32[128]{0:T(128)}, f32[128]{0:T(128)S(1)}, u32[]{:S(2)}) copy-start(f32[128]{0:T(128)S(1)} %get-tuple-element.136) | copy-start | bytes 1540
  581.9 9.8 %copy-start.31 = (f32[128]{0:T(128)}, f32[128]{0:T(128)S(1)}, u32[]{:S(2)}) copy-start(f32[128]{0:T(128)S(1)} %get-tuple-element.142) | copy-start | bytes 1540
  (24 other events, 99.4 us)
Sparse Core Ops, SparseCore 0:
  10.2 134.3 all-gather.6
  146.7 77.0 all-gather.8
  314.9 161.6 reduce-scatter.4
  480.6 107.8 reduce-scatter.2

commit v2 on v1

v2 whole, which is shorter than its diff:
```python
import functools
import math

import jax
import jax.numpy as jnp
from jax import lax
from jax.experimental import pallas as pl
from jax.experimental.pallas import tpu as pltpu
from jax.sharding import Mesh
from jax.sharding import PartitionSpec as P

HEADS = 8
HEAD_DIM = 256
ROT = 64

EPS = 1e-05
MASKED = -1e30
ROT_BASE = 10000.0
ROOT_HALF = 0.7071067811865476
INV_ROOT_TAU = 0.3989422804014327

WIDE = ("z", "y", "core")
CHIPS = ("z", "y")
TAIL = 8
BLOCK = 256
VMEM_BYTES = 58 * 1024 * 1024
f32 = jnp.float32
bf16 = jnp.bfloat16


def rotary_tables(places):
    halves = ROT // 2
    inverse = ROT_BASE ** (-2.0 * jnp.arange(halves, dtype=f32) / ROT)
    angles = places.astype(f32)[:, None] * inverse[None, :]
    return (jnp.cos(angles), jnp.sin(angles))


def norm_stats(values):
    average = jnp.mean(values, axis=-1, keepdims=True)
    centered = values - average
    variance = jnp.mean(centered * centered, axis=-1, keepdims=True)
    scale = lax.rsqrt(variance + EPS)
    return (centered * scale, scale)


def swap(part, axis):
    return lax.ppermute(part, axis, [(0, 1), (1, 0)])


def pair(index, own, other, axis=0):
    return jnp.where(
        index == 0, jnp.stack([own, other], axis=axis), jnp.stack([other, own], axis=axis)
    )


def dot(a, b, dims, out=f32):
    return lax.dot_general(a, b, (dims, ((), ())), preferred_element_type=f32).astype(out)


NN = ((1,), (0,))
NT = ((1,), (1,))
TN = ((0,), (0,))


def pick(array, index, axis=0):
    return lax.dynamic_index_in_dim(array, index, axis, keepdims=False)


def gather_rows(own):
    return lax.all_gather(own, CHIPS, axis=0, tiled=True)


def rows_kernel(d, own, other, w, out, sums):
    @pl.when(pl.program_id(0) == 0)
    def _():
        sums[...] = jnp.zeros_like(sums)

    half = out.shape[0] // 2
    width = own.shape[2]
    for j in range(own.shape[0]):
        cols = slice(j * width, (j + 1) * width)
        mine, got = own[j].astype(f32), other[j].astype(f32)
        bias = mine[half : half + 1] + got[half : half + 1]
        for at in range(2):
            rows = slice(at * half, (at + 1) * half)
            grad = jnp.where(d[0] == at, mine[:half], got[:half])
            out[rows, cols] = grad
            weight = w[rows, cols].astype(f32)
            sums[rows, 0:1] += jnp.sum(weight * grad, axis=1, keepdims=True)
            sums[rows, 1:2] += jnp.sum(weight * bias, axis=1, keepdims=True)


def weight_rows(name, d, own, other, w, width, order=()):
    devices, height, columns = own.shape
    rows = w.shape[0]
    group = math.gcd(2048 // width, devices)
    blocks = devices // group
    shape = (group, height, width)
    at = lambda i: (lax.rem(i, blocks), 0, lax.div(i, blocks))
    grad, sums = call(
        rows_kernel,
        name,
        blocks * (columns // width),
        [
            (d, "scalars"),
            (own, shape, at),
            (other, shape, at),
            (w, (rows, group * width), lambda i: (0, i)),
        ],
        [((rows, w.shape[1]), f32, (rows, group * width), lambda i: (0, i)), ((rows, 2), f32, None)],
        order=order,
    )
    return (grad, sums[:, 0], sums[:, 1])


def half_kernel(mine, got, row, out):
    total = (mine[...].astype(f32) + got[...].astype(f32)).astype(bf16)
    tail = (out.shape[0], out.shape[1] - total.shape[1], out.shape[2])
    row = jnp.broadcast_to(row[...][None], tail).astype(bf16)
    out[...] = jnp.concatenate([total, row], axis=1)


def half_sum(name, mine, send, row, order):
    devices, rows, width = mine.shape
    return call(
        half_kernel,
        name,
        1,
        [(mine, None), (swap(send, "dp"), None), (row.reshape(1, width), None)],
        [((devices, rows + TAIL, width), bf16, None)],
        order=order,
    )[0]


def gate(value, *others):
    spec = pl.BlockSpec(memory_space=pl.ANY)
    return pl.pallas_call(
        lambda *refs: None,
        in_specs=[spec] * (1 + len(others)),
        out_specs=spec,
        out_shape=jax.ShapeDtypeStruct(value.shape, value.dtype),
        input_output_aliases={0: 0},
        name="gate",
    )(value, *others)


def scatter_rows(part):
    return lax.psum_scatter(part, CHIPS, scatter_dimension=0, tiled=True).astype(f32)


def call(kernel, name, grid, ins, outs, scratch=(), order=(), flops=0):
    def whole(shape):
        return pl.BlockSpec(shape, lambda i: (0,) * len(shape))

    def blocked(shape, block, at=None):
        if block == "scalars":
            return pl.BlockSpec(memory_space=pltpu.SMEM)
        if block is None:
            return whole(shape)
        return pl.BlockSpec(block, at or (lambda i: (i,) + (0,) * (len(block) - 1)))

    def run(*refs):
        kernel(*refs[: len(ins)], *refs[len(ins) + len(order) :])

    arrays = [entry[0] for entry in ins]
    moved = sum(a.size * a.dtype.itemsize for a in arrays)
    moved += sum(functools.reduce(lambda p, n: p * n, o[0], 1) * o[1].dtype.itemsize for o in outs)
    return pl.pallas_call(
        run,
        grid=(grid,),
        in_specs=[blocked(entry[0].shape, *entry[1:]) for entry in ins]
        + [pl.BlockSpec(memory_space=pl.ANY)] * len(order),
        out_specs=[blocked(o[0], *o[2:]) for o in outs],
        out_shape=[jax.ShapeDtypeStruct(o[0], o[1]) for o in outs],
        scratch_shapes=list(scratch),
        compiler_params=pltpu.CompilerParams(
            vmem_limit_bytes=VMEM_BYTES, dimension_semantics=("arbitrary",)
        ),
        cost_estimate=pl.CostEstimate(flops=flops, bytes_accessed=moved, transcendentals=0),
        name=name,
    )(*arrays, *order)


def turn(half, c_ref, down_ref, up_ref, way):
    width, step = half.shape[-1], ROT // 2
    ahead = pltpu.roll(half, width - step, 1) * down_ref
    behind = pltpu.roll(half, step, 1) * up_ref
    return half * c_ref + way * (behind - ahead)


def part_rows(at, total, own, other):
    rows = own.shape[0]
    first = at[0] == 0
    own[...] = jnp.where(first, total[:rows], total[rows:])
    other[...] = jnp.where(first, total[rows:], total[:rows])


def front_kernel(x, ok, norms, wuo, wux, wqo, wqx, bu, bq, cos, low, high, h1, h2, acto, actx, slo, slx, q, k, v):
    n, _ = norm_stats(x[...].astype(f32))
    first = (n * norms[0:1, :] + norms[1:2, :]).astype(bf16)
    second = (n * norms[2:3, :] + norms[3:4, :]).astype(bf16)
    h1[...] = first
    h2[...] = second
    for at, (w, act, slope) in enumerate(((wuo, acto, slo), (wux, actx, slx))):
        upper = dot(second, w[...], NN) + bu[at : at + 1, :]
        cdf = 0.5 * (1.0 + lax.erf(upper * ROOT_HALF))
        act[...] = (upper * cdf * ok[...]).astype(bf16)
        slope[...] = cdf + upper * jnp.exp(-0.5 * upper * upper) * INV_ROOT_TAU
    for at, w in enumerate((wqo, wqx)):
        joined = dot(first, w[...], NN) + bq[at : at + 1, :]
        wide = joined.shape[1] // 3
        cols = slice(at * wide, (at + 1) * wide)
        tables = (cos[:, cols], low[:, cols], high[:, cols])
        q[:, cols] = turn(joined[:, :wide], *tables, 1.0).astype(bf16)
        k[:, cols] = turn(joined[:, wide : 2 * wide], *tables, 1.0).astype(bf16)
        v[:, cols] = joined[:, 2 * wide :].astype(bf16)


def weights_of(q, k, row_place, col_place, scale):
    scores = dot(q, k, NT) * scale
    return jnp.where(col_place <= row_place, scores, MASKED)


def attend_kernel(scale, q, k, v, ok, row_place, col_place, att, lse):
    rows = q.shape[0]
    step = min(BLOCK, rows)
    for start in range(0, rows, step):
        mine, seen = slice(start, start + step), slice(0, start + step)
        scores = weights_of(q[mine, :], k[seen, :], row_place[mine, :], col_place[:, seen], scale)
        top = jnp.max(scores, axis=1, keepdims=True)
        raised = jnp.exp(scores - top)
        total = jnp.sum(raised, axis=1, keepdims=True)
        weights = (raised * (1.0 / total)).astype(bf16)
        att[mine, :] = (dot(weights, v[seen, :], NN) * ok[mine, :]).astype(bf16)
        lse[mine, :] = top + jnp.log(total)


def attend_back_kernel(scale, q, k, v, ga, lse, row_place, col_place, cos, low, high, gjo, gjx, sums, gk, gv):
    rows = q.shape[0]
    step = min(BLOCK, rows)
    gk[...] = jnp.zeros_like(gk)
    gv[...] = jnp.zeros_like(gv)
    wide = q.shape[1] // 2
    for start in range(0, rows, step):
        mine, seen = slice(start, start + step), slice(0, start + step)
        scores = weights_of(q[mine, :], k[seen, :], row_place[mine, :], col_place[:, seen], scale)
        soft = jnp.exp(scores - lse[mine, :])
        g_soft = dot(ga[mine, :], v[seen, :], NT)
        product = soft * g_soft
        delta = jnp.sum(product, axis=1, keepdims=True)
        g_scores = (product - soft * delta).astype(bf16)
        gk[seen, :] += dot(g_scores, q[mine, :], TN)
        gv[seen, :] += dot(soft.astype(bf16), ga[mine, :], TN)
        g_q = dot(g_scores, k[seen, :], NN) * scale
        for at, out in enumerate((gjo, gjx)):
            cols = slice(at * wide, (at + 1) * wide)
            tables = (cos[mine, cols], low[mine, cols], high[mine, cols])
            out[mine, :wide] = turn(g_q[:, cols], *tables, -1.0).astype(bf16)
    for start in range(0, rows, step):
        mine = slice(start, start + step)
        for at, out in enumerate((gjo, gjx)):
            cols = slice(at * wide, (at + 1) * wide)
            tables = (cos[mine, cols], low[mine, cols], high[mine, cols])
            out[mine, wide : 2 * wide] = turn(gk[mine, cols] * scale, *tables, -1.0).astype(bf16)
            out[mine, 2 * wide :] = gv[mine, cols].astype(bf16)
    for at, out in enumerate((gjo, gjx)):
        sums[at : at + 1, :] = jnp.sum(out[...].astype(f32), axis=0, keepdims=True)


def out_kernel(acto, actx, att, wo, wx, wd, out, done):
    total = dot(acto[...], wo[...], NN) + dot(actx[...], wx[...], NN) + dot(att[...], wd[...], NN)
    out[...] = total.astype(bf16)
    done[...] = jnp.zeros_like(done)


def back_kernel(c, ok, slo, slx, wo, wx, wd, guo, gux, ga, sums, sum_go):
    @pl.when(pl.program_id(0) == 0)
    def _():
        sums[...] = jnp.zeros_like(sums)
        sum_go[...] = jnp.zeros_like(sum_go)

    grad = jnp.where(ok[...] > 0, c[...], jnp.zeros((), bf16))
    for at, (w, slope, gu) in enumerate(((wo, slo, guo), (wx, slx, gux))):
        low = (dot(grad, w[...], NT) * slope[...]).astype(bf16)
        gu[...] = low
        sums[at : at + 1, :] += jnp.sum(low.astype(f32), axis=0, keepdims=True)
    ga[...] = dot(grad, wd[...], NT, bf16)
    sum_go[...] += jnp.sum(grad.astype(f32), axis=0, keepdims=True)


def in_kernel(gjo, gjx, guo, gux, wqo, wqx, wuo, wux, norms, out, done):
    one = dot(gjo[...], wqo[...], NT) + dot(gjx[...], wqx[...], NT)
    two = dot(guo[...], wuo[...], NT) + dot(gux[...], wux[...], NT)
    out[...] = (one * norms[0:1, :] + two * norms[2:3, :]).astype(bf16)
    done[...] = jnp.zeros_like(done)


def turned_kernel(left, right, *rest):
    total = dot(left[...], right[...], TN)
    if len(rest) == 2:
        total = total + rest[0][...].astype(f32)
    rest[-1][...] = total.astype(bf16)


def turned_half_kernel(d, left, right, got, mine, other):
    total = (dot(left[...], right[...], TN) + got[...].astype(f32)).astype(bf16)
    rows = mine.shape[1]
    for i in range(mine.shape[0]):
        at = slice(2 * i * rows, 2 * (i + 1) * rows)
        part_rows(d, total[at], mine.at[i], other.at[i])


def turned_product(name, left, right, got=None, start=0, count=None, halves=None, order=()):
    depth = left.shape[0]
    count = count or left.shape[1] - start
    width = right.shape[1]
    block = math.gcd(BLOCK, count)
    first = start // block
    ins = [(left, (depth, block), lambda i: (0, first + i)), (right, None)]
    if got is not None:
        ins.append((got, (block, width)))
    if halves:
        place, rows = halves
        blocks = (block // (2 * rows), rows, width)
        return call(
            turned_half_kernel,
            name,
            count // block,
            [(place, "scalars")] + ins,
            [((count // (2 * rows), rows, width), bf16, blocks)] * 2,
            order=order,
            flops=2 * depth * count * width,
        )
    return call(
        turned_kernel,
        name,
        count // block,
        ins,
        [((count, width), bf16, (block, width))],
        order=order,
        flops=2 * depth * count * width,
    )[0]


def local(
    tokens,
    lengths,
    gain_one,
    shift_one,
    w_qkv,
    b_qkv,
    w_dense,
    b_dense,
    gain_two,
    shift_two,
    w_up,
    b_up,
    w_down,
    b_down,
    cotangent,
):
    _, span, D = tokens.shape
    chips = lax.axis_size("z") * 2
    W = chips * 2
    G = chips // HEADS
    L = span * W
    R = w_qkv.shape[0]
    H2 = R // 2
    HK = HEAD_DIM // 2
    QW = 3 * HK
    FW = w_down.shape[0]
    FF = w_up.shape[1]
    z, y, k, d = (lax.axis_index(a) for a in ("z", "y", "core", "dp"))
    chip = z * 2 + y
    me = chip * 2 + k
    head = chip // G

    vectors = (gain_one, shift_one, gain_two, shift_two, b_qkv, b_dense, b_down, b_up)
    small = jnp.concatenate(vectors)
    small = jnp.pad(small, (0, TAIL * QW - small.shape[0])).reshape(1, TAIL, QW)
    u_rows = pick(w_up.reshape(2, H2, W, FW), d).transpose(1, 0, 2)
    u_got = lax.all_to_all(u_rows, WIDE, 0, 0, tiled=True)
    q_rows = pick(w_qkv.reshape(2, H2, 3, HEADS, 2, HK), d)
    q_rows = q_rows.transpose(2, 3, 0, 1, 4).reshape(HEADS, 1, 2, H2, QW)
    q_rows = jnp.broadcast_to(q_rows, (HEADS, G, 2, H2, QW)).reshape(W, H2, QW)
    q_sent = jnp.concatenate([q_rows, jnp.broadcast_to(small, (W, TAIL, QW))], axis=1)
    q_got = lax.all_to_all(q_sent, WIDE, 0, 0, tiled=True)

    def whole(got):
        return pair(d, got, swap(got, "dp"), axis=1).reshape(D, got.shape[-1])

    wu_own = whole(u_got)
    wu_other = swap(wu_own, "core")
    wq_own = whole(q_got[:, :H2])
    wq_other = swap(wq_own, "core")
    small_all = q_got[:, H2:].reshape(W, TAIL * QW)
    pieces = []
    start = 0
    for piece in vectors:
        pieces.append(small_all[:, start : start + piece.shape[0]].astype(f32))
        start += piece.shape[0]
    g1, s1, g2, s2, bq_all, bd_all, bo_all = (piece.reshape(-1) for piece in pieces[:-1])
    bu_all = pieces[-1]
    bu_own, bu_other = pick(bu_all, me), pick(bu_all, me + 1 - 2 * k)
    bq_head = pick(bq_all.reshape(3, HEADS, 2, HK), head, 1)
    bq_own, bq_other = (pick(bq_head, at, 1).reshape(QW) for at in (k, 1 - k))
    if G == 1:
        wd = jnp.concatenate([w_dense, swap(w_dense, "core")], axis=0)
    else:
        wd = pick(lax.all_gather(w_dense, WIDE).reshape(HEADS, 2, HK, D), head)
        wd = jnp.concatenate([pick(wd, k), pick(wd, 1 - k)], axis=0)
    w_down_other = swap(w_down, "core")
    wo = jnp.concatenate([w_down, w_down_other, wd], axis=0)

    def own_seq(array):
        return jnp.concatenate(
            [pick(array, k), swap(pick(array, 1 - k), "core")], axis=0
        )

    x_chip = own_seq(tokens)
    c_chip = own_seq(cotangent)
    length = pick(lengths, k)
    x_all = gather_rows(x_chip)
    c_all = gather_rows(c_chip)

    both = jnp.arange(2, dtype=jnp.int32)
    in_chip = ((both ^ k)[:, None] * span + jnp.arange(span, dtype=jnp.int32)).reshape(2 * span)
    place = (jnp.arange(chips, dtype=jnp.int32)[:, None] * (2 * span) + in_chip).reshape(L)
    place_chip = chip * (2 * span) + in_chip

    cosine, sine = rotary_tables(place)
    flat = jnp.zeros((L, HK - ROT), f32)
    nil = jnp.zeros((L, ROT // 2), f32)
    at_core = ((both ^ k) == 0)[None, :, None]

    def table(turned, otherwise):
        return jnp.where(at_core, turned[:, None, :], otherwise).reshape(L, 2 * HK)

    cos_t = table(jnp.concatenate([cosine, cosine, flat + 1.0], axis=1), 1.0)
    low_t = table(jnp.concatenate([sine, nil, flat], axis=1), 0.0)
    high_t = table(jnp.concatenate([nil, sine, flat], axis=1), 0.0)
    ok = (place < length).astype(f32).reshape(L, 1)
    row_place = place.reshape(L, 1)
    col_place = jnp.where(place < length, place, jnp.int32(2**30)).reshape(1, L)

    rows = 4 * span
    steps = L // rows
    norms = jnp.stack([g1, s1, g2, s2])
    h1, h2, act_own, act_other, slope_own, slope_other, queries, keys, values = call(
        front_kernel,
        "norm_up_qkv",
        steps,
        [
            (x_all, (rows, D)),
            (ok, (rows, 1)),
            (norms, None),
            (wu_own, None),
            (wu_other, None),
            (wq_own, None),
            (wq_other, None),
            (jnp.stack([bu_own, bu_other]), None),
            (jnp.stack([bq_own, bq_other]), None),
            (cos_t, (rows, 2 * HK)),
            (low_t, (rows, 2 * HK)),
            (high_t, (rows, 2 * HK)),
        ],
        [((L, D), bf16, (rows, D))] * 2
        + [((L, FW), bf16, (rows, FW))] * 2
        + [((L, FW), f32, (rows, FW))] * 2
        + [((L, HEAD_DIM), bf16, (rows, HEAD_DIM))] * 3,
        flops=2 * L * D * (2 * FW + 2 * QW),
    )
    score_scale = HEAD_DIM ** (-0.5)
    mine = (place // (L // G) == chip % G)[:, None]
    attended, lse = call(
        functools.partial(attend_kernel, score_scale),
        "attend",
        1,
        [(a, None) for a in (queries, keys, values, ok, row_place, col_place)],
        [((L, HEAD_DIM), bf16, None), ((L, 1), f32, None)],
        flops=4 * L * L * HEAD_DIM,
    )
    if G > 1:
        attended = jnp.where(mine, attended, jnp.zeros((), bf16))

    mixed_part, mixed_done = call(
        out_kernel,
        "dense_down",
        steps,
        [
            (act_own, (rows, FW)),
            (act_other, (rows, FW)),
            (attended, (rows, HEAD_DIM)),
            (w_down, None),
            (w_down_other, None),
            (wd, None),
        ],
        [((L, D), bf16, (rows, D)), ((8, 128), f32, None)],
        flops=2 * L * D * (2 * FW + HEAD_DIM),
    )
    mixed_sum = scatter_rows(mixed_part)

    gu_own, gu_other, ga, gb_u, gb_o = call(
        back_kernel,
        "back_dense_down",
        steps,
        [
            (c_all, (rows, D)),
            (ok, (rows, 1)),
            (slope_own, (rows, FW)),
            (slope_other, (rows, FW)),
            (w_down, None),
            (w_down_other, None),
            (wd, None),
        ],
        [
            ((L, FW), bf16, (rows, FW)),
            ((L, FW), bf16, (rows, FW)),
            ((L, HEAD_DIM), bf16, (rows, HEAD_DIM)),
            ((2, FW), f32, None),
            ((1, D), f32, None),
        ],
        order=(mixed_done,),
        flops=2 * L * D * (2 * FW + HEAD_DIM),
    )
    if G > 1:
        ga = jnp.where(mine, ga, jnp.zeros((), bf16))
    at_d = d.astype(jnp.int32).reshape(1)
    part = FW // 2 if FW % 256 == 0 else FW
    up_other = turned_product("grad_up_other", h2, gu_other)
    down_other = turned_product("grad_down_other", act_other, c_all, count=part, order=(up_other,))
    gb_o = jnp.concatenate(
        [lax.dynamic_slice_in_dim(gb_o[0], at * R, R) for at in (me, me + 1 - 2 * k)]
    )

    def over_cores(own, other):
        return own + swap(other, "core")

    bias = over_cores(
        jnp.concatenate([gb_u[0], gb_o[:R]]), jnp.concatenate([gb_u[1], gb_o[R:]])
    )
    gb_u, gb_o = bias[:FW], bias[FW:]

    up_mine, up_send = turned_product(
        "grad_up_own",
        h2,
        gu_own,
        got=swap(up_other, "core"),
        halves=(at_d, H2),
        order=(down_other, bias),
    )

    gj_own, gj_other, gb_j = call(
        functools.partial(attend_back_kernel, score_scale),
        "back_attend",
        1,
        [
            (a, None)
            for a in (queries, keys, values, ga, lse, row_place, col_place, cos_t, low_t, high_t)
        ],
        [((L, QW), bf16, None), ((L, QW), bf16, None), ((2, QW), f32, None)],
        scratch=[pltpu.VMEM((L, HEAD_DIM), f32)] * 2,
        order=(up_mine,),
        flops=10 * L * L * HEAD_DIM,
    )

    qkv_other = turned_product("grad_qkv_other", h1, gj_other)
    down_own = turned_product(
        "grad_down_own", act_own, c_all, got=swap(down_other, "core"), count=part,
        order=(qkv_other,),
    )
    down_dp = swap(down_own, "dp")
    gb_q = over_cores(gb_j[0], gb_j[1])
    qkv_mine, qkv_send = turned_product(
        "grad_qkv_own",
        h1,
        gj_own,
        got=swap(qkv_other, "core"),
        halves=(at_d, H2),
        order=(down_own, gb_q),
    )
    up_half = half_sum("half_up", up_mine, up_send, gb_u, (qkv_mine,))

    f_part, f_done = call(
        in_kernel,
        "back_up_qkv",
        steps,
        [
            (gj_own, (rows, QW)),
            (gj_other, (rows, QW)),
            (gu_own, (rows, FW)),
            (gu_other, (rows, FW)),
            (wq_own, None),
            (wq_other, None),
            (wu_own, None),
            (wu_other, None),
            (norms, None),
        ],
        [((L, D), bf16, (rows, D)), ((8, 128), f32, None)],
        order=(up_half,),
        flops=2 * L * D * (2 * FW + 2 * QW),
    )
    qkv_half = half_sum("half_qkv", qkv_mine, qkv_send, gb_q, (f_done,))
    f_sum = scatter_rows(gate(f_part, mixed_sum, qkv_half))
    up_got = lax.all_to_all(up_half, WIDE, 0, 0, tiled=True)
    last = (qkv_half,)
    if part < FW:
        rest_other = turned_product(
            "grad_down_other2", act_other, c_all, start=part, order=last
        )
        last = (rest_other,)
    dense_other = turned_product("grad_dense_other", attended, c_all, start=HK, order=last)
    dense_got = swap(dense_other, "core") if G == 1 else jnp.zeros_like(dense_other)
    downs = [(down_own, down_dp)]
    last = (dense_other,)
    if part < FW:
        rest_own = turned_product(
            "grad_down_own2", act_own, c_all, got=swap(rest_other, "core"), start=part,
            order=last,
        )
        downs.append((rest_own, swap(rest_own, "dp")))
        last = (rest_own,)
    dense_own = turned_product(
        "grad_dense_own", attended, c_all, got=dense_got, count=HK, order=last
    )
    ok_chip = (place_chip < length)[:, None]
    x_chip_f = x_chip.astype(f32)
    mixed_chip = jnp.where(ok_chip, x_chip_f + mixed_sum + (bd_all + bo_all), 0.0).astype(bf16)

    def own_positions(rows):
        return pair(k, rows[:span], swap(rows[span:], "core"))

    mixed = own_positions(mixed_chip)

    n_chip, r_chip = norm_stats(x_chip_f)
    grad_x = r_chip * (
        f_sum
        - jnp.mean(f_sum, axis=-1, keepdims=True)
        - n_chip * jnp.mean(f_sum * n_chip, axis=-1, keepdims=True)
    )
    go_chip = jnp.where(ok_chip, c_chip.astype(f32), 0.0)
    token_grad = own_positions((go_chip + grad_x).astype(bf16))

    gw_down = jnp.concatenate([own.astype(f32) + got.astype(f32) for own, got in downs], axis=0)
    if G > 1:
        dense = pair(k, dense_own, dense_other).reshape(1, HEAD_DIM, D).astype(f32)
        at_head = (jnp.arange(HEADS) == head)[:, None, None]
        dense = jnp.where(at_head, dense, 0.0).reshape(D, D)
        dense_own = lax.psum_scatter(dense, WIDE, scatter_dimension=0, tiled=True).astype(bf16)
    gw_dense = dense_own.astype(f32) + swap(dense_own, "dp").astype(f32)

    def norm_grads(product, shift_grad, gain, shift):
        return ((product - shift.astype(f32) * shift_grad) / gain.astype(f32), shift_grad)

    def tail_of(own, other):
        return own[:, H2].astype(f32) + other[:, H2].astype(f32)

    qkv_got = lax.all_to_all(gate(qkv_half, up_got, dense_own), WIDE, 0, 0, tiled=True)
    up_dp = swap(up_got, "dp")
    qkv_dp = swap(qkv_got, "dp")
    gw_up, up_sum, up_shift = weight_rows("rows_up", at_d, up_got, up_dp, w_up, FW)
    gg2, gs2 = norm_grads(up_sum, up_shift, gain_two, shift_two)
    gb_up = pick(tail_of(up_got, up_dp), me)
    gb_out = gb_o + swap(gb_o, "dp")
    gb_q_all = tail_of(qkv_got, qkv_dp)
    gb_q_all = gb_q_all.reshape(HEADS, G, 2, 3, HK).sum(1).transpose(2, 0, 1, 3).reshape(3 * D)
    if G == 1:
        gw_q, q_sum, q_shift = weight_rows(
            "rows_qkv", at_d, qkv_got, qkv_dp, w_qkv, HK, order=(mixed, token_grad)
        )
    else:
        gw_q = pair(d, qkv_got[:, :H2], qkv_dp[:, :H2]).astype(f32)
        gw_q = gw_q.reshape(2, HEADS, G, 2, H2, 3, HK).sum(2)
        gw_q = gw_q.transpose(0, 3, 4, 1, 2, 5).reshape(R, 3 * D)
        wf = w_qkv.astype(f32)
        q_sum, q_shift = jnp.sum(wf * gw_q, axis=1), jnp.sum(wf * gb_q_all[None, :], axis=1)
    gg1, gs1 = norm_grads(q_sum, q_shift, gain_one, shift_one)
    gb_qkv = lax.dynamic_slice_in_dim(gb_q_all, me * 3 * R, 3 * R)
    return (
        mixed,
        token_grad,
        gg1,
        gs1,
        gw_q,
        gb_qkv,
        gw_dense,
        gb_out,
        gg2,
        gs2,
        gw_up,
        gb_up,
        gw_down,
        gb_out,
    )


def solution(mesh):
    dp, wide = mesh.shape["dp"], mesh.shape["wide"]
    split = Mesh(mesh.devices.reshape(dp, wide // 4, 2, 2), ("dp",) + WIDE)
    rows = P("dp", WIDE, None)
    mat, vec = P(WIDE, None), P(WIDE)
    in_specs = (rows, P("dp"), vec, vec, mat, vec, mat, vec, vec, vec, mat, vec, mat, vec, rows)
    out_specs = (rows, rows, vec, vec, mat, vec, mat, vec, vec, vec, mat, vec, mat, vec)
    return jax.shard_map(local, mesh=split, in_specs=in_specs, out_specs=out_specs, check_vma=False)
```

time: 603 us -> 451 us (0.75)
  Pallas kernels: 0 us -> 144 us
  blocking collectives: 111 us -> 0 us
  matrix products: 88 us -> 0 us
  other arithmetic: 91.5 us -> 36.6 us
  waiting for transfers between devices: 193 us -> 155 us
  local copies, waits for them, and re-layouts: 70.3 us -> 39 us
  starting transfers between devices: 29.8 us -> 53.3 us
    pallas_call x0 -> x22, Pallas kernels: none -> 144 us  [the longest x20 144 us: call(): pl.pallas_call(run, grid=(grid,), in_specs=[blocked(entry[0].shape, *entr...]
    all_gather x1 -> x0, blocking collectives: 111 us -> none  [local(): small_all = lax.all_gather(small, WIDE)]
    dot_general x14 -> x0, matrix products: 88 us -> none  [dot(): lax.dot_general(a, b, (dims, ((), ())), preferred_element_type=f32)]
    all_to_all x3 -> x4, waiting for transfers between devices: 93.7 us -> 47.2 us  [the longest x1 23.5 us: local(): u_got = lax.all_to_all(u_rows, WIDE, 0, 0, tiled=True)]
    convert_element_type x9 -> x4, other arithmetic: 21.1 us -> 5.46 us  [the longest x1 2.12 us: scatter_rows(): lax.psum_scatter(part, CHIPS, scatter_dimension=0, tiled=True).astype(f32)]
    all_to_all x3 -> x4, starting transfers between devices: 22.9 us -> 35.2 us  [the longest x1 16.7 us: local(): lax.all_to_all(gate(qkv_half, up_got, dense_own), WIDE, 0, 0, tiled=True)]
    reduce_sum x2 -> x1, other arithmetic: 11.8 us -> 0.29 us  [norm_stats(): variance = jnp.mean(centered * centered, axis=-1, keepdims=True)]
    ppermute x8 -> x25, starting transfers between devices: 6.7 us -> 17.4 us  [swap(): return lax.ppermute(part, axis, [(0, 1), (1, 0)])]
  transfers between devices with their start and end apart: 15 -> 33, of which waited for: 7 -> 15; matrix products, arithmetic and copies ran while one was open for 31% -> 13% of each run, Pallas kernels for 0% -> 31%
where the time goes in v2:
time: 451 us; the launch traced here: 443 us
  waiting for transfers between devices  155 us (34%)
  Pallas kernels  144 us (32%)
  starting transfers between devices  53.3 us (12%)
  local copies, waits for them, and re-layouts  39 us (9%)
  other arithmetic  36.6 us (8%)
  between operations  14.7 us (3%)
    pallas_call x20, Pallas kernels, call(): pl.pallas_call(run, grid=(grid,), in_specs=[blocked(entry[0].shape, *entr...  144 us
    ppermute x25, waiting for transfers between devices, swap(): return lax.ppermute(part, axis, [(0, 1), (1, 0)])  65.9 us
    all_gather x2, waiting for transfers between devices, gather_rows(): return lax.all_gather(own, CHIPS, axis=0, tiled=True)  30.9 us
    all_to_all x1, waiting for transfers between devices, local(): u_got = lax.all_to_all(u_rows, WIDE, 0, 0, tiled=True)  23.5 us
    all_to_all x1, waiting for transfers between devices, local(): q_got = lax.all_to_all(q_sent, WIDE, 0, 0, tiled=True)  22.3 us
    ppermute x25, starting transfers between devices, swap(): return lax.ppermute(part, axis, [(0, 1), (1, 0)])  17.4 us
    unnamed x98, local copies, waits for them, and re-layouts  17.2 us
    all_to_all x1, starting transfers between devices, local(): lax.all_to_all(gate(qkv_half, up_got, dense_own), WIDE, 0, 0, tiled=True)  16.7 us
  transfers between devices with their start and end apart: 33, of which 15 were waited for; matrix products, arithmetic and copies ran while one was open for 13% of the time, Pallas kernels for 31%

profile of v2, /device:TPU:0, one launch (start us, length us, event | category | flops | bytes accessed | tf_op | source)
XLA Modules:
  0.0 443.2 jit_solution(2288515282637487302)
XLA Ops:
  16.1 7.5 %all-to-all-start.1 = ((bf16[16,64,512]{2,1,0:T(8,128)(2,1)}), bf16[16,64,512]{2,1,0:T(8,128)(2,1)S(1)}, u32[]{:S(2)}, u32[]{:S(2)}) async-start(bf16[16,64,512]{2,1,0:T(8,128)(2,1)} %bitcast.95), calls=%async_computation.1 | async-start | bytes 2097152 | tf_op jit(solution)/shard_map/all_to_all | solution.py:382
  38.0 23.5 %all-to-all-done.1 = bf16[16,64,512]{2,1,0:T(8,128)(2,1)S(1)} async-done(((bf16[16,64,512]{2,1,0:T(8,128)(2,1)}), bf16[16,64,512]{2,1,0:T(8,128)(2,1)S(1)}, u32[]{:S(2)}, u32[]{:S(2)}) %all-to-all-start.1) | async-done | bytes 1048608 | tf_op jit(solution)/shard_map/all_to_all | solution.py:382
  61.4 7.0 %all-to-all-start = ((bf16[16,72,384]{2,1,0:T(8,128)(2,1)}), bf16[16,72,384]{2,1,0:T(8,128)(2,1)S(1)}, u32[]{:S(2)}, u32[]{:S(2)}) async-start(bf16[16,72,384]{2,1,0:T(8,128)(2,1)} %pad_maximum_fusion.1), calls=%async_computation | async-start | bytes 1769472 | tf_op jit(solution)/shard_map/all_to_all | solution.py:387
  80.6 22.3 %all-to-all-done = bf16[16,72,384]{2,1,0:T(8,128)(2,1)S(1)} async-done(((bf16[16,72,384]{2,1,0:T(8,128)(2,1)}), bf16[16,72,384]{2,1,0:T(8,128)(2,1)S(1)}, u32[]{:S(2)}, u32[]{:S(2)}) %all-to-all-start) | async-done | bytes 884768 | tf_op jit(solution)/shard_map/all_to_all | solution.py:387
  110.3 14.0 %collective-permute-done.3 = bf16[16,64,384]{2,1,0:T(8,128)(2,1)} collective-permute-done((bf16[16,64,384]{2,1,0:T(8,128)(2,1)}, bf16[16,64,384]{2,1,0:T(8,128)(2,1)}, u32[]{:S(2)}, u32[]{:S(2)}) %collective-permute-start.3) | collective-permute-done | bytes 786464 | tf_op jit(solution)/shard_map/ppermute | solution.py:47
  130.9 19.8 %norm_up_qkv.1 = (bf16[1024,2048]{1,0:T(8,128)(2,1)}, bf16[1024,2048]{1,0:T(8,128)(2,1)}, bf16[1024,512]{1,0:T(8,128)(2,1)}, bf16[1024,512]{1,0:T(8,128)(2,1)}, ...) custom-call(bf16[1024,2048]{1,0:T(8,128)(2,1)} %all-gather.3.cloned., ...), custom_call_target="tpu_custom_call" | custom-call | flops 7516192768 | bytes 30977024 | tf_op jit(solution)/shard_map/norm_up_qkv/pallas_call | solution.py:168
  150.7 4.8 %attend.1 = (bf16[1024,256]{1,0:T(8,128)(2,1)}, f32[1024,1]{1,0:T(8,128)}) custom-call(bf16[1024,256]{1,0:T(8,128)(2,1)} %get-tuple-element.47.refs_0_, bf16[1024,256]{1,0:T(8,128)(2,1)} %get-tuple-element.48.refs_1_, bf16[1024,256]{1,0:T(8,128)(2,1)} %get-tuple-element.49.refs_2_, f32[1024,1]{1,0:T(8,128)} %compare_convert_fusion.refs_1_.refs_3_, ...), custom_call_target="tpu_custom_call" | custom-call | flops 1073741824 | bytes 2113536 | tf_op jit(solution)/shard_map/attend/pallas_call | solution.py:168
  155.5 10.7 %dense_down.1 = (bf16[1024,2048]{1,0:T(8,128)(2,1)}, f32[8,128]{1,0:T(8,128)}) custom-call(bf16[1024,512]{1,0:T(8,128)(2,1)} %get-tuple-element.45.refs_0_, bf16[1024,512]{1,0:T(8,128)(2,1)} %get-tuple-element.46.refs_1_.refs_0_, bf16[1024,256]{1,0:T(8,128)(2,1)} %get-tuple-element.50.refs_2_.refs_0_, bf16[512,2048]{1,0:T(8,128)(2,1)} %refs_4_.1, ...), custom_call_target="tpu_custom_call" | custom-call | flops 5368709120 | bytes 12062720 | tf_op jit(solution)/shard_map/dense_down/pallas_call | solution.py:168
  166.3 30.9 %all-gather.5.cloned.1.call-done.refs_0_.refs_1_ = bf16[1024,2048]{1,0:T(8,128)(2,1)} async-done(((bf16[128,2048]{1,0:T(8,128)(2,1)}), bf16[1024,2048]{1,0:T(8,128)(2,1)}) %all-gather.5.cloned.1.call-update) | async-done | bytes 4194320 | tf_op jit(solution)/shard_map/all_gather | solution.py:70
  197.1 10.8 %back_dense_down.1 = (bf16[1024,512]{1,0:T(8,128)(2,1)}, bf16[1024,512]{1,0:T(8,128)(2,1)}, bf16[1024,256]{1,0:T(8,128)(2,1)}, f32[2,512]{1,0:T(2,128)}, f32[1,2048]{1,0:T(1,128)}) custom-call(bf16[1024,2048]{1,0:T(8,128)(2,1)} %all-gather.5.cloned.1.call-done.refs_0_.refs_1_, f32[1024,1]{1,0:T(8,128)} %compare_convert_fusion.refs_1_.refs_3_, ...), custom_call_target="tpu_custom_call" | custom-call | flops 5368709120 | bytes 16269312 | tf_op jit(solution)/shard_map/back_dense_down/pallas_call | solution.py:168
  208.0 8.1 %grad_up_other.1.refs_2_ = bf16[2048,512]{1,0:T(8,128)(2,1)} custom-call(bf16[1024,2048]{1,0:T(8,128)(2,1)} %get-tuple-element.57.refs_0_.refs_1_, bf16[1024,512]{1,0:T(8,128)(2,1)} %get-tuple-element.59.refs_1_.refs_3_), custom_call_target="tpu_custom_call" | custom-call | flops 2147483648 | bytes 7340032 | tf_op jit(solution)/shard_map/grad_up_other/pallas_call | solution.py:168
  217.4 4.7 %grad_down_other.1.refs_4_ = bf16[256,2048]{1,0:T(8,128)(2,1)} custom-call(bf16[1024,512]{1,0:T(8,128)(2,1)} %get-tuple-element.46.refs_1_.refs_0_, bf16[1024,2048]{1,0:T(8,128)(2,1)} %all-gather.5.cloned.1.call-done.refs_0_.refs_1_, bf16[2048,512]{1,0:T(8,128)(2,1)} %grad_up_other.1.refs_2_), custom_call_target="tpu_custom_call" | custom-call | flops 1073741824 | bytes 6291456 | tf_op jit(solution)/shard_map/grad_down_other/pallas_call | solution.py:168
  224.1 8.8 %grad_up_own.1 = (bf16[16,64,512]{2,1,0:T(8,128)(2,1)}, bf16[16,64,512]{2,1,0:T(8,128)(2,1)}) custom-call(s32[1]{0:T(128)} %bitcast.22.refs_0_, bf16[1024,2048]{1,0:T(8,128)(2,1)} %get-tuple-element.57.refs_0_.refs_1_, bf16[1024,512]{1,0:T(8,128)(2,1)} %get-tuple-element.58.refs_2_, bf16[2048,512]{1,0:T(8,128)(2,1)} %copy-done.13, ...), custom_call_target="tpu_custom_call" | custom-call | flops 2147483648 | bytes 9437188 | tf_op jit(solution)/shard_map/grad_up_own/pallas_call | solution.py:168
  232.8 7.9 %back_attend.1 = (bf16[1024,384]{1,0:T(8,128)(2,1)}, bf16[1024,384]{1,0:T(8,128)(2,1)}, f32[2,384]{1,0:T(2,128)}) custom-call(bf16[1024,256]{1,0:T(8,128)(2,1)} %get-tuple-element.47.refs_0_, bf16[1024,256]{1,0:T(8,128)(2,1)} %get-tuple-element.48.refs_1_, bf16[1024,256]{1,0:T(8,128)(2,1)} %get-tuple-element.49.refs_2_, ...), custom_call_target="tpu_custom_call" | custom-call | flops 2684354560 | bytes 6831104 | tf_op jit(solution)/shard_map/back_attend/pallas_call | solution.py:168
  240.7 8.1 %grad_qkv_other.1.refs_3_ = bf16[2048,384]{1,0:T(8,128)(2,1)} custom-call(bf16[1024,2048]{1,0:T(8,128)(2,1)} %get-tuple-element.66.refs_0_.refs_1_, bf16[1024,384]{1,0:T(8,128)(2,1)} %get-tuple-element.64.refs_1_), custom_call_target="tpu_custom_call" | custom-call | flops 1610612736 | bytes 6553600 | tf_op jit(solution)/shard_map/grad_qkv_other/pallas_call | solution.py:168
  254.6 4.9 %grad_down_own.1.refs_4_ = bf16[256,2048]{1,0:T(8,128)(2,1)} custom-call(bf16[1024,512]{1,0:T(8,128)(2,1)} %get-tuple-element.45.refs_0_, bf16[1024,2048]{1,0:T(8,128)(2,1)} %all-gather.5.cloned.1.call-done.refs_0_.refs_1_, bf16[256,2048]{1,0:T(8,128)(2,1)} %copy-done.19, bf16[2048,384]{1,0:T(8,128)(2,1)} %grad_qkv_other.1.refs_3_), custom_call_target="tpu_custom_call" | custom-call | flops 1073741824 | bytes 7340032 | tf_op jit(solution)/shard_map/grad_down_own/pallas_call | solution.py:168
  261.3 8.5 %grad_qkv_own.1 = (bf16[16,64,384]{2,1,0:T(8,128)(2,1)}, bf16[16,64,384]{2,1,0:T(8,128)(2,1)}) custom-call(s32[1]{0:T(128)} %bitcast.22.refs_0_, bf16[1024,2048]{1,0:T(8,128)(2,1)} %get-tuple-element.66.refs_0_.refs_1_, bf16[1024,384]{1,0:T(8,128)(2,1)} %get-tuple-element.63.refs_2_.refs_0_, bf16[2048,384]{1,0:T(8,128)(2,1)} %copy-done.15, ...), custom_call_target="tpu_custom_call" | custom-call | flops 1610612736 | bytes 8126468 | tf_op jit(solution)/shard_map/grad_qkv_own/pallas_call | solution.py:168
  272.3 3.2 collective-permute-done.11.refs_1_
  279.3 14.3 %back_up_qkv.1 = (bf16[1024,2048]{1,0:T(8,128)(2,1)}, f32[8,128]{1,0:T(8,128)}) custom-call(bf16[1024,384]{1,0:T(8,128)(2,1)} %get-tuple-element.63.refs_2_.refs_0_, bf16[1024,384]{1,0:T(8,128)(2,1)} %get-tuple-element.64.refs_1_, bf16[1024,512]{1,0:T(8,128)(2,1)} %get-tuple-element.58.refs_2_, bf16[1024,512]{1,0:T(8,128)(2,1)} %get-tuple-element.59.refs_1_.refs_3_, ...), custom_call_target="tpu_custom_call" | custom-call | flops 7516192768 | bytes 15241216 | tf_op jit(solution)/shard_map/back_up_qkv/pallas_call | solution.py:168
  299.2 4.1 all-to-all-start.2
  305.6 4.6 %grad_down_other2.1.refs_2_ = bf16[256,2048]{1,0:T(8,128)(2,1)} custom-call(bf16[1024,512]{1,0:T(8,128)(2,1)} %get-tuple-element.46.refs_1_.refs_0_, bf16[1024,2048]{1,0:T(8,128)(2,1)} %all-gather.5.cloned.1.call-done.refs_0_.refs_1_, bf16[16,72,384]{2,1,0:T(8,128)(2,1)} %half_qkv.1.refs_2_.refs_0_), custom_call_target="tpu_custom_call" | custom-call | flops 1073741824 | bytes 6291456 | tf_op jit(solution)/shard_map/grad_down_other2/pallas_call | solution.py:168
  311.4 3.8 grad_dense_other.1.refs_3_
  315.3 14.3 %collective-permute-done.21 = f32[128]{0:T(128)S(1)} collective-permute-done((f32[128]{0:T(128)S(1)}, f32[128]{0:T(128)S(1)}, u32[]{:S(2)}, u32[]{:S(2)}) %collective-permute-start.21) | collective-permute-done | bytes 544 | tf_op jit(solution)/shard_map/ppermute | solution.py:47
  330.7 4.9 %grad_down_own2.1.refs_3_ = bf16[256,2048]{1,0:T(8,128)(2,1)} custom-call(bf16[1024,512]{1,0:T(8,128)(2,1)} %get-tuple-element.45.refs_0_, bf16[1024,2048]{1,0:T(8,128)(2,1)} %all-gather.5.cloned.1.call-done.refs_0_.refs_1_, bf16[256,2048]{1,0:T(8,128)(2,1)} %copy-done.18, bf16[128,2048]{1,0:T(8,128)(2,1)} %grad_dense_other.1.refs_3_), custom_call_target="tpu_custom_call" | custom-call | flops 1073741824 | bytes 7340032 | tf_op jit(solution)/shard_map/grad_down_own2/pallas_call | solution.py:168
  337.8 3.9 grad_dense_own.1.refs_2_
  346.4 16.7 %all-to-all-start.3 = ((bf16[16,72,384]{2,1,0:T(8,128)(2,1)}), bf16[16,72,384]{2,1,0:T(8,128)(2,1)S(1)}, u32[]{:S(2)}, u32[]{:S(2)}) async-start(bf16[16,72,384]{2,1,0:T(8,128)(2,1)} %gate.3), calls=%async_computation.5 | async-start | bytes 1769472 | tf_op jit(solution)/shard_map/all_to_all | solution.py:658
  365.6 7.6 %collective-permute-done.20 = bf16[128,2048]{1,0:T(8,128)(2,1)} collective-permute-done((bf16[128,2048]{1,0:T(8,128)(2,1)}, bf16[128,2048]{1,0:T(8,128)(2,1)}, u32[]{:S(2)}, u32[]{:S(2)}) %collective-permute-start.20) | collective-permute-done | bytes 524320 | tf_op jit(solution)/shard_map/ppermute | solution.py:47
  379.7 17.2 %collective-permute-done.22.refs_2_ = bf16[16,72,512]{2,1,0:T(8,128)(2,1)S(1)} collective-permute-done((bf16[16,72,512]{2,1,0:T(8,128)(2,1)}, bf16[16,72,512]{2,1,0:T(8,128)(2,1)S(1)}, u32[]{:S(2)}, u32[]{:S(2)}) %collective-permute-start.22) | collective-permute-done | bytes 1179680 | tf_op jit(solution)/shard_map/ppermute | solution.py:47
  398.0 5.3 %rows_up.1 = (f32[128,8192]{1,0:T(8,128)}, f32[128,2]{1,0:T(8,128)}) custom-call(s32[1]{0:T(128)} %bitcast.22.refs_0_, bf16[16,72,512]{2,1,0:T(8,128)(2,1)} %copy-done, bf16[16,72,512]{2,1,0:T(8,128)(2,1)} %copy-done.16, bf16[128,8192]{1,0:T(8,128)(2,1)} %refs_3_.5), custom_call_target="tpu_custom_call" | custom-call | bytes 8651780 | tf_op jit(solution)/shard_map/rows_up/pallas_call | solution.py:168
  406.9 11.2 %reduce-scatter.5.cloned.1.call-done = bf16[128,2048]{1,0:T(8,128)(2,1)} async-done(((bf16[1024,2048]{1,0:T(8,128)(2,1)}), bf16[128,2048]{1,0:T(8,128)(2,1)}) %reduce-scatter.5.cloned.1.call-update) | async-done | bytes 524304 | tf_op jit(solution)/shard_map/reduce_scatter | solution.py:148
  422.2 3.6 collective-permute-done.19.refs_2_
  429.2 5.1 %rows_qkv.1 = (f32[128,6144]{1,0:T(8,128)}, f32[128,2]{1,0:T(8,128)}) custom-call(s32[1]{0:T(128)} %bitcast.22.refs_0_, bf16[16,72,384]{2,1,0:T(8,128)(2,1)} %copy-done.8, bf16[16,72,384]{2,1,0:T(8,128)(2,1)} %collective-permute-done.19.refs_2_, bf16[128,6144]{1,0:T(8,128)(2,1)} %refs_3_.4, bf16[2,64,2048]{2,1,0:T(8,128)(2,1)} %maximum_select_fusion.2.refs_4_, ...), custom_call_target="tpu_custom_call" | custom-call | bytes 6489092 | tf_op jit(solution)/shard_map/rows_qkv/pallas_call | solution.py:168
  (254 shorter events, 106.5 us)
Async XLA Ops:
  7.2 123.7 %all-gather.3.cloned.1.call-start = ((), (), s32[]{:S(2)}) async-start(), calls=%async_computation.6 | async-start | bytes 4718592 | tf_op jit(solution)/shard_map/all_gather | solution.py:70
  8.5 1.7 collective-permute-start
  16.1 45.3 %all-to-all-start.1 = ((bf16[16,64,512]{2,1,0:T(8,128)(2,1)}), bf16[16,64,512]{2,1,0:T(8,128)(2,1)S(1)}, u32[]{:S(2)}, u32[]{:S(2)}) async-start(bf16[16,64,512]{2,1,0:T(8,128)(2,1)} %bitcast.95), calls=%async_computation.1 | async-start | bytes 2097152 | tf_op jit(solution)/shard_map/all_to_all | solution.py:382
  23.5 173.6 %all-gather.5.cloned.1.call-start = ((), (), s32[]{:S(2)}) async-start(), calls=%async_computation.8 | async-start | bytes 4718592 | tf_op jit(solution)/shard_map/all_gather | solution.py:70
  25.1 81.0 %collective-permute-start.6 = (bf16[128,2048]{1,0:T(8,128)(2,1)}, bf16[128,2048]{1,0:T(8,128)(2,1)}, u32[]{:S(2)}, u32[]{:S(2)}) collective-permute-start(bf16[128,2048]{1,0:T(8,128)(2,1)} %param.21), channel_id=1, source_target_pairs={{0,1},{1,0},{2,3},{3,2},{4,5},{5,4},{6,7},{7,6},{8,9},{9,8},{10,11... | collective-permute-start | bytes 1572872 | tf_op jit(solution)/shard_map/ppermute | solution.py:47
  25.2 130.3 %collective-permute-start.5 = (bf16[512,2048]{1,0:T(8,128)(2,1)}, bf16[512,2048]{1,0:T(8,128)(2,1)}, u32[]{:S(2)}, u32[]{:S(2)}) collective-permute-start(bf16[512,2048]{1,0:T(8,128)(2,1)} %refs_4_.1), channel_id=1, source_target_pairs={{0,1},{1,0},{2,3},{3,2},{4,5},{5,4},{6,7},{7,6},{8,9},{9,8},{10,11... | collective-permute-start | bytes 6291464 | tf_op jit(solution)/shard_map/ppermute | solution.py:47
  61.4 41.6 %all-to-all-start = ((bf16[16,72,384]{2,1,0:T(8,128)(2,1)}), bf16[16,72,384]{2,1,0:T(8,128)(2,1)S(1)}, u32[]{:S(2)}, u32[]{:S(2)}) async-start(bf16[16,72,384]{2,1,0:T(8,128)(2,1)} %pad_maximum_fusion.1), calls=%async_computation | async-start | bytes 1769472 | tf_op jit(solution)/shard_map/all_to_all | solution.py:387
  68.4 228.6 %reduce-scatter.3.cloned.1.call-start = ((), (), s32[]{:S(2)}) async-start(), calls=%async_computation.7 | async-start | bytes 4718592 | tf_op jit(solution)/shard_map/reduce_scatter | solution.py:148
  75.9 32.3 %collective-permute-start.1 = (bf16[16,64,512]{2,1,0:T(8,128)(2,1)S(1)}, bf16[16,64,512]{2,1,0:T(8,128)(2,1)}, u32[]{:S(2)}, u32[]{:S(2)}) collective-permute-start(bf16[16,64,512]{2,1,0:T(8,128)(2,1)S(1)} %all-to-all-done.1), channel_id=1, source_target_pairs={{0,16},{16,0},{1,17},{17,1},{2,18},{18,2},{3,19},{19,3},{4,20},{20... | collective-permute-start | bytes 3145736 | tf_op jit(solution)/shard_map/ppermute | solution.py:47
  104.4 19.9 %collective-permute-start.3 = (bf16[16,64,384]{2,1,0:T(8,128)(2,1)}, bf16[16,64,384]{2,1,0:T(8,128)(2,1)}, u32[]{:S(2)}, u32[]{:S(2)}) collective-permute-start(bf16[16,64,384]{2,1,0:T(8,128)(2,1)} %get-tuple-element.87), channel_id=1, source_target_pairs={{0,16},{16,0},{1,17},{17,1},{2,18},{18,2},{3,19},{19,3},{4,20},{20... | collective-permute-start | bytes 2359304 | tf_op jit(solution)/shard_map/ppermute | solution.py:47
  110.1 20.8 %collective-permute-start.2 = (bf16[2048,512]{1,0:T(8,128)(2,1)S(1)}, bf16[2048,512]{1,0:T(8,128)(2,1)}, u32[]{:S(2)}, u32[]{:S(2)}) collective-permute-start(bf16[2048,512]{1,0:T(8,128)(2,1)S(1)} %bitcast.97), channel_id=1, source_target_pairs={{0,1},{1,0},{2,3},{3,2},{4,5},{5,4},{6,7},{7,6},{8,9},{9,8},{10,11... | collective-permute-start | bytes 6291464 | tf_op jit(solution)/shard_map/ppermute | solution.py:47
  126.2 3.5 collective-permute-start.4
  166.2 251.9 %reduce-scatter.5.cloned.1.call-start = ((), (), s32[]{:S(2)}) async-start(), calls=%async_computation.9 | async-start | bytes 4718592 | tf_op jit(solution)/shard_map/reduce_scatter | solution.py:148
  216.1 6.6 %collective-permute-start.9 = (bf16[2048,512]{1,0:T(8,128)(2,1)}, bf16[2048,512]{1,0:T(8,128)(2,1)S(1)}, u32[]{:S(2)}, u32[]{:S(2)}) collective-permute-start(bf16[2048,512]{1,0:T(8,128)(2,1)} %grad_up_other.1.refs_2_), channel_id=1, source_target_pairs={{0,1},{1,0},{2,3},{3,2},{4,5},{5,4},{6,7},{7,6},{8,9},{9,8},{10,11... | collective-permute-start | bytes 6291464 | tf_op jit(solution)/shard_map/ppermute | solution.py:47
  216.8 5.3 %collective-permute-start.10 = (f32[640]{0:T(1024)S(1)}, f32[640]{0:T(1024)S(1)}, u32[]{:S(2)}, u32[]{:S(2)}) collective-permute-start(f32[640]{0:T(1024)S(1)} %pad_maximum_fusion.5), channel_id=1, source_target_pairs={{0,1},{1,0},{2,3},{3,2},{4,5},{5,4},{6,7},{7,6},{8,9},{9,8},{10,11... | collective-permute-start | bytes 7688 | tf_op jit(solution)/shard_map/ppermute | solution.py:47
  248.8 11.3 %collective-permute-start.12 = (bf16[2048,384]{1,0:T(8,128)(2,1)}, bf16[2048,384]{1,0:T(8,128)(2,1)S(1)}, u32[]{:S(2)}, u32[]{:S(2)}) collective-permute-start(bf16[2048,384]{1,0:T(8,128)(2,1)} %grad_qkv_other.1.refs_3_), channel_id=1, source_target_pairs={{0,1},{1,0},{2,3},{3,2},{4,5},{5,4},{6,7},{7,6},{8,9},{9,8},{10,11... | collective-permute-start | bytes 4718600 | tf_op jit(solution)/shard_map/ppermute | solution.py:47
  248.9 4.8 %collective-permute-start.13 = (bf16[256,2048]{1,0:T(8,128)(2,1)S(1)}, bf16[256,2048]{1,0:T(8,128)(2,1)S(1)}, u32[]{:S(2)}, u32[]{:S(2)}) collective-permute-start(bf16[256,2048]{1,0:T(8,128)(2,1)S(1)} %copy-done.7), channel_id=1, source_target_pairs={{0,1},{1,0},{2,3},{3,2},{4,5},{5,4},{6,7},{7,6},{8,9},{9,8},{10,11... | collective-permute-start | bytes 3145736 | tf_op jit(solution)/shard_map/ppermute | solution.py:47
  249.3 26.2 %collective-permute-start.11 = (bf16[16,64,512]{2,1,0:T(8,128)(2,1)}, bf16[16,64,512]{2,1,0:T(8,128)(2,1)S(1)}, u32[]{:S(2)}, u32[]{:S(2)}) collective-permute-start(bf16[16,64,512]{2,1,0:T(8,128)(2,1)} %get-tuple-element.65), channel_id=1, source_target_pairs={{0,16},{16,0},{1,17},{17,1},{2,18},{18,2},{3,19},{19,3},{4,20},{20... | collective-permute-start | bytes 3145736 | tf_op jit(solution)/shard_map/ppermute | solution.py:47
  250.8 8.7 %collective-permute-start.14 = (f32[384]{0:T(512)S(1)}, f32[384]{0:T(512)S(1)}, u32[]{:S(2)}, u32[]{:S(2)}) collective-permute-start(f32[384]{0:T(512)S(1)} %get-tuple-element.82), channel_id=1, source_target_pairs={{0,1},{1,0},{2,3},{3,2},{4,5},{5,4},{6,7},{7,6},{8,9},{9,8},{10,11... | collective-permute-start | bytes 4616 | tf_op jit(solution)/shard_map/ppermute | solution.py:47
  269.7 23.9 %collective-permute-start.15 = (bf16[16,64,384]{2,1,0:T(8,128)(2,1)}, bf16[16,64,384]{2,1,0:T(8,128)(2,1)S(1)}, u32[]{:S(2)}, u32[]{:S(2)}) collective-permute-start(bf16[16,64,384]{2,1,0:T(8,128)(2,1)} %get-tuple-element.70), channel_id=1, source_target_pairs={{0,16},{16,0},{1,17},{17,1},{2,18},{18,2},{3,19},{19,3},{4,20},{20... | collective-permute-start | bytes 2359304 | tf_op jit(solution)/shard_map/ppermute | solution.py:47
  299.2 46.2 %all-to-all-start.2 = ((bf16[16,72,512]{2,1,0:T(8,128)(2,1)}), bf16[16,72,512]{2,1,0:T(8,128)(2,1)S(1)}, u32[]{:S(2)}, u32[]{:S(2)}) async-start(bf16[16,72,512]{2,1,0:T(8,128)(2,1)} %half_up.1.refs_9_), calls=%async_computation.4 | async-start | bytes 2359296 | tf_op jit(solution)/shard_map/all_to_all | solution.py:605
  304.1 38.2 %collective-permute-start.23 = (bf16[256,2048]{1,0:T(8,128)(2,1)S(1)}, bf16[256,2048]{1,0:T(8,128)(2,1)S(1)}, u32[]{:S(2)}, u32[]{:S(2)}) collective-permute-start(bf16[256,2048]{1,0:T(8,128)(2,1)S(1)} %copy-done.1), channel_id=1, source_target_pairs={{0,16},{16,0},{1,17},{17,1},{2,18},{18,2},{3,19},{19,3},{4,20},{20... | collective-permute-start | bytes 3145736 | tf_op jit(solution)/shard_map/ppermute | solution.py:47
  310.3 19.4 %collective-permute-start.18 = (bf16[256,2048]{1,0:T(8,128)(2,1)}, bf16[256,2048]{1,0:T(8,128)(2,1)S(1)}, u32[]{:S(2)}, u32[]{:S(2)}) collective-permute-start(bf16[256,2048]{1,0:T(8,128)(2,1)} %grad_down_other2.1.refs_2_), channel_id=1, source_target_pairs={{0,1},{1,0},{2,3},{3,2},{4,5},{5,4},{6,7},{7,6},{8,9},{9,8},{10,11... | collective-permute-start | bytes 3145736 | tf_op jit(solution)/shard_map/ppermute | solution.py:47
  310.6 19.0 %collective-permute-start.21 = (f32[128]{0:T(128)S(1)}, f32[128]{0:T(128)S(1)}, u32[]{:S(2)}, u32[]{:S(2)}) collective-permute-start(f32[128]{0:T(128)S(1)} %slice.107), channel_id=1, source_target_pairs={{0,16},{16,0},{1,17},{17,1},{2,18},{18,2},{3,19},{19,3},{4,20},{20... | collective-permute-start | bytes 1544 | tf_op jit(solution)/shard_map/ppermute | solution.py:47
  315.2 21.8 %collective-permute-start.17 = (bf16[128,2048]{1,0:T(8,128)(2,1)}, bf16[128,2048]{1,0:T(8,128)(2,1)S(1)}, u32[]{:S(2)}, u32[]{:S(2)}) collective-permute-start(bf16[128,2048]{1,0:T(8,128)(2,1)} %grad_dense_other.1.refs_3_), channel_id=1, source_target_pairs={{0,1},{1,0},{2,3},{3,2},{4,5},{5,4},{6,7},{7,6},{8,9},{9,8},{10,11... | collective-permute-start | bytes 1572872 | tf_op jit(solution)/shard_map/ppermute | solution.py:47
  335.5 39.8 %collective-permute-start.24 = (bf16[256,2048]{1,0:T(8,128)(2,1)}, bf16[256,2048]{1,0:T(8,128)(2,1)}, u32[]{:S(2)}, u32[]{:S(2)}) collective-permute-start(bf16[256,2048]{1,0:T(8,128)(2,1)} %grad_down_own2.1.refs_3_), channel_id=1, source_target_pairs={{0,16},{16,0},{1,17},{17,1},{2,18},{18,2},{3,19},{19,3},{4,20},{20... | collective-permute-start | bytes 3145736 | tf_op jit(solution)/shard_map/ppermute | solution.py:47
  341.8 31.4 %collective-permute-start.20 = (bf16[128,2048]{1,0:T(8,128)(2,1)}, bf16[128,2048]{1,0:T(8,128)(2,1)}, u32[]{:S(2)}, u32[]{:S(2)}) collective-permute-start(bf16[128,2048]{1,0:T(8,128)(2,1)} %grad_dense_own.1.refs_2_), channel_id=1, source_target_pairs={{0,16},{16,0},{1,17},{17,1},{2,18},{18,2},{3,19},{19,3},{4,20},{20... | collective-permute-start | bytes 1572872 | tf_op jit(solution)/shard_map/ppermute | solution.py:47
  346.4 59.0 %all-to-all-start.3 = ((bf16[16,72,384]{2,1,0:T(8,128)(2,1)}), bf16[16,72,384]{2,1,0:T(8,128)(2,1)S(1)}, u32[]{:S(2)}, u32[]{:S(2)}) async-start(bf16[16,72,384]{2,1,0:T(8,128)(2,1)} %gate.3), calls=%async_computation.5 | async-start | bytes 1769472 | tf_op jit(solution)/shard_map/all_to_all | solution.py:658
  364.1 32.9 %collective-permute-start.22 = (bf16[16,72,512]{2,1,0:T(8,128)(2,1)}, bf16[16,72,512]{2,1,0:T(8,128)(2,1)S(1)}, u32[]{:S(2)}, u32[]{:S(2)}) collective-permute-start(bf16[16,72,512]{2,1,0:T(8,128)(2,1)} %copy-done), channel_id=1, source_target_pairs={{0,16},{16,0},{1,17},{17,1},{2,18},{18,2},{3,19},{19,3},{4,20},{20... | collective-permute-start | bytes 3538952 | tf_op jit(solution)/shard_map/ppermute | solution.py:47
  405.4 20.3 %collective-permute-start.19 = (bf16[16,72,384]{2,1,0:T(8,128)(2,1)S(1)}, bf16[16,72,384]{2,1,0:T(8,128)(2,1)}, u32[]{:S(2)}, u32[]{:S(2)}) collective-permute-start(bf16[16,72,384]{2,1,0:T(8,128)(2,1)S(1)} %all-to-all-done.3.refs_1_), channel_id=1, source_target_pairs={{0,16},{16,0},{1,17},{17,1},{2,18},{18,2},{3,19},{19,3},{4,20},{20... | collective-permute-start | bytes 2654216 | tf_op jit(solution)/shard_map/ppermute | solution.py:47
  421.5 6.0 %collective-permute-start.16 = (bf16[64,2048]{1,0:T(8,128)(2,1)S(1)}, bf16[64,2048]{1,0:T(8,128)(2,1)S(1)}, u32[]{:S(2)}, u32[]{:S(2)}) collective-permute-start(bf16[64,2048]{1,0:T(8,128)(2,1)S(1)} %get-tuple-element.91), channel_id=1, source_target_pairs={{0,1},{1,0},{2,3},{3,2},{4,5},{5,4},{6,7},{7,6},{8,9},{9,8},{10,11... | collective-permute-start | bytes 786440 | tf_op jit(solution)/shard_map/ppermute | solution.py:47
  421.6 6.7 %collective-permute-start.7 = (bf16[64,2048]{1,0:T(8,128)(2,1)S(1)}, bf16[64,2048]{1,0:T(8,128)(2,1)S(1)}, u32[]{:S(2)}, u32[]{:S(2)}) collective-permute-start(bf16[64,2048]{1,0:T(8,128)(2,1)S(1)} %get-tuple-element.95), channel_id=1, source_target_pairs={{0,1},{1,0},{2,3},{3,2},{4,5},{5,4},{6,7},{7,6},{8,9},{9,8},{10,11... | collective-permute-start | bytes 786440 | tf_op jit(solution)/shard_map/ppermute | solution.py:47
  (44 other events, 547.4 us)
Sparse Core Ops, SparseCore 0:
  11.1 111.3 all-gather.2
  124.6 72.4 all-gather.4
  200.8 86.3 reduce-scatter.2
  299.3 118.8 reduce-scatter.4

commit v3 on v2

--- a/solution.py
+++ b/solution.py
@@ -145,7 +145,7 @@
 
 
 def scatter_rows(part):
-    return lax.psum_scatter(part, CHIPS, scatter_dimension=0, tiled=True).astype(f32)
+    return lax.psum_scatter(part, CHIPS, scatter_dimension=0, tiled=True)
 
 
 def call(kernel, name, grid, ins, outs, scratch=(), order=(), flops=0):
@@ -526,9 +526,8 @@
     if G > 1:
         ga = jnp.where(mine, ga, jnp.zeros((), bf16))
     at_d = d.astype(jnp.int32).reshape(1)
-    part = FW // 2 if FW % 256 == 0 else FW
+    part = 128 if FW % 128 == 0 else FW
     up_other = turned_product("grad_up_other", h2, gu_other)
-    down_other = turned_product("grad_down_other", act_other, c_all, count=part, order=(up_other,))
     gb_o = jnp.concatenate(
         [lax.dynamic_slice_in_dim(gb_o[0], at * R, R) for at in (me, me + 1 - 2 * k)]
     )
@@ -540,15 +539,6 @@
         jnp.concatenate([gb_u[0], gb_o[:R]]), jnp.concatenate([gb_u[1], gb_o[R:]])
     )
     gb_u, gb_o = bias[:FW], bias[FW:]
-
-    up_mine, up_send = turned_product(
-        "grad_up_own",
-        h2,
-        gu_own,
-        got=swap(up_other, "core"),
-        halves=(at_d, H2),
-        order=(down_other, bias),
-    )
 
     gj_own, gj_other, gb_j = call(
         functools.partial(attend_back_kernel, score_scale),
@@ -560,16 +550,33 @@
         ],
         [((L, QW), bf16, None), ((L, QW), bf16, None), ((2, QW), f32, None)],
         scratch=[pltpu.VMEM((L, HEAD_DIM), f32)] * 2,
-        order=(up_mine,),
+        order=(up_other,),
         flops=10 * L * L * HEAD_DIM,
     )
 
-    qkv_other = turned_product("grad_qkv_other", h1, gj_other)
+    up_mine, up_send = turned_product(
+        "grad_up_own",
+        h2,
+        gu_own,
+        got=swap(up_other, "core"),
+        halves=(at_d, H2),
+        order=(gj_own, bias),
+    )
+    qkv_other = turned_product("grad_qkv_other", h1, gj_other, order=(up_mine,))
+    down_other = turned_product("grad_down_other", act_other, c_all, count=part, order=(qkv_other,))
     down_own = turned_product(
         "grad_down_own", act_own, c_all, got=swap(down_other, "core"), count=part,
-        order=(qkv_other,),
+        order=(down_other,),
     )
     down_dp = swap(down_own, "dp")
+    last = (down_own,)
+    if part < FW:
+        rest_other = turned_product(
+            "grad_down_other2", act_other, c_all, start=part, order=last
+        )
+        last = (rest_other,)
+    up_half = half_sum("half_up", up_mine, up_send, gb_u, last)
+    up_got = lax.all_to_all(up_half, WIDE, 0, 0, tiled=True)
     gb_q = over_cores(gb_j[0], gb_j[1])
     qkv_mine, qkv_send = turned_product(
         "grad_qkv_own",
@@ -577,9 +584,8 @@
         gj_own,
         got=swap(qkv_other, "core"),
         halves=(at_d, H2),
-        order=(down_own, gb_q),
-    )
-    up_half = half_sum("half_up", up_mine, up_send, gb_u, (qkv_mine,))
+        order=(up_half, gb_q),
+    )
 
     f_part, f_done = call(
         in_kernel,
@@ -597,18 +603,12 @@
             (norms, None),
         ],
         [((L, D), bf16, (rows, D)), ((8, 128), f32, None)],
-        order=(up_half,),
+        order=(qkv_mine, down_dp),
         flops=2 * L * D * (2 * FW + 2 * QW),
     )
     qkv_half = half_sum("half_qkv", qkv_mine, qkv_send, gb_q, (f_done,))
-    f_sum = scatter_rows(gate(f_part, mixed_sum, qkv_half))
-    up_got = lax.all_to_all(up_half, WIDE, 0, 0, tiled=True)
+    f_sum = scatter_rows(gate(f_part, mixed_sum, qkv_half, up_got)).astype(f32)
     last = (qkv_half,)
-    if part < FW:
-        rest_other = turned_product(
-            "grad_down_other2", act_other, c_all, start=part, order=last
-        )
-        last = (rest_other,)
     dense_other = turned_product("grad_dense_other", attended, c_all, start=HK, order=last)
     dense_got = swap(dense_other, "core") if G == 1 else jnp.zeros_like(dense_other)
     downs = [(down_own, down_dp)]
@@ -625,7 +625,7 @@
     )
     ok_chip = (place_chip < length)[:, None]
     x_chip_f = x_chip.astype(f32)
-    mixed_chip = jnp.where(ok_chip, x_chip_f + mixed_sum + (bd_all + bo_all), 0.0).astype(bf16)
+    mixed_chip = jnp.where(ok_chip, x_chip_f + mixed_sum.astype(f32) + (bd_all + bo_all), 0.0).astype(bf16)
 
     def own_positions(rows):
         return pair(k, rows[:span], swap(rows[span:], "core"))
@@ -641,7 +641,6 @@
     go_chip = jnp.where(ok_chip, c_chip.astype(f32), 0.0)
     token_grad = own_positions((go_chip + grad_x).astype(bf16))
 
-    gw_down = jnp.concatenate([own.astype(f32) + got.astype(f32) for own, got in downs], axis=0)
     if G > 1:
         dense = pair(k, dense_own, dense_other).reshape(1, HEAD_DIM, D).astype(f32)
         at_head = (jnp.arange(HEADS) == head)[:, None, None]
@@ -655,19 +654,18 @@
     def tail_of(own, other):
         return own[:, H2].astype(f32) + other[:, H2].astype(f32)
 
-    qkv_got = lax.all_to_all(gate(qkv_half, up_got, dense_own), WIDE, 0, 0, tiled=True)
+    qkv_got = lax.all_to_all(gate(qkv_half, up_got), WIDE, 0, 0, tiled=True)
     up_dp = swap(up_got, "dp")
     qkv_dp = swap(qkv_got, "dp")
-    gw_up, up_sum, up_shift = weight_rows("rows_up", at_d, up_got, up_dp, w_up, FW)
+    gw_up, up_sum, up_shift = weight_rows("rows_up", at_d, up_got, up_dp, w_up, FW, order=(qkv_got,))
     gg2, gs2 = norm_grads(up_sum, up_shift, gain_two, shift_two)
     gb_up = pick(tail_of(up_got, up_dp), me)
-    gb_out = gb_o + swap(gb_o, "dp")
+    gw_down = jnp.concatenate([own.astype(f32) + gate(got, gw_up).astype(f32) for own, got in downs], axis=0)
+    gb_out = gb_o + gate(swap(gate(gb_o, qkv_got), "dp"), qkv_dp)
     gb_q_all = tail_of(qkv_got, qkv_dp)
     gb_q_all = gb_q_all.reshape(HEADS, G, 2, 3, HK).sum(1).transpose(2, 0, 1, 3).reshape(3 * D)
     if G == 1:
-        gw_q, q_sum, q_shift = weight_rows(
-            "rows_qkv", at_d, qkv_got, qkv_dp, w_qkv, HK, order=(mixed, token_grad)
-        )
+        gw_q, q_sum, q_shift = weight_rows("rows_qkv", at_d, qkv_got, qkv_dp, w_qkv, HK)
     else:
         gw_q = pair(d, qkv_got[:, :H2], qkv_dp[:, :H2]).astype(f32)
         gw_q = gw_q.reshape(2, HEADS, G, 2, H2, 3, HK).sum(2)

time: 451 us -> 453 us (level)
  the two profiles are of different devices: /device:TPU:0 before, /device:TPU:13 now
where the time goes in v3:
time: 453 us; the launch traced here: 445 us
  waiting for transfers between devices  173 us (38%)
  Pallas kernels  144 us (32%)
  starting transfers between devices  42.3 us (9%)
  local copies, waits for them, and re-layouts  37.6 us (8%)
  other arithmetic  33.2 us (7%)
  between operations  14.7 us (3%)
    pallas_call x20, Pallas kernels, call(): pl.pallas_call(run, grid=(grid,), in_specs=[blocked(entry[0].shape, *entr...  144 us
    ppermute x25, waiting for transfers between devices, swap(): return lax.ppermute(part, axis, [(0, 1), (1, 0)])  87.1 us
    all_to_all x1, waiting for transfers between devices, local(): q_got = lax.all_to_all(q_sent, WIDE, 0, 0, tiled=True)  32 us
    all_to_all x1, waiting for transfers between devices, local(): u_got = lax.all_to_all(u_rows, WIDE, 0, 0, tiled=True)  29.4 us
    ppermute x25, starting transfers between devices, swap(): return lax.ppermute(part, axis, [(0, 1), (1, 0)])  19.8 us
    unnamed x94, local copies, waits for them, and re-layouts  18.3 us
    all_gather x2, waiting for transfers between devices, gather_rows(): return lax.all_gather(own, CHIPS, axis=0, tiled=True)  18.1 us
  transfers between devices with their start and end apart: 33, of which 14 were waited for; matrix products, arithmetic and copies ran while one was open for 12% of the time, Pallas kernels for 32%

profile of v3, /device:TPU:13, one launch (start us, length us, event | category | flops | bytes accessed | tf_op | source)
XLA Modules:
  0.0 445.4 jit_solution(5338173765185703935)
XLA Ops:
  16.3 6.4 %all-to-all-start.1 = ((bf16[16,64,512]{2,1,0:T(8,128)(2,1)}), bf16[16,64,512]{2,1,0:T(8,128)(2,1)}, u32[]{:S(2)}, u32[]{:S(2)}) async-start(bf16[16,64,512]{2,1,0:T(8,128)(2,1)} %bitcast.94), calls=%async_computation.1 | async-start | bytes 2097152 | tf_op jit(solution)/shard_map/all_to_all | solution.py:382
  33.5 29.4 %all-to-all-done.1 = bf16[16,64,512]{2,1,0:T(8,128)(2,1)} async-done(((bf16[16,64,512]{2,1,0:T(8,128)(2,1)}), bf16[16,64,512]{2,1,0:T(8,128)(2,1)}, u32[]{:S(2)}, u32[]{:S(2)}) %all-to-all-start.1) | async-done | bytes 1048608 | tf_op jit(solution)/shard_map/all_to_all | solution.py:382
  62.9 4.7 %all-to-all-start = ((bf16[16,72,384]{2,1,0:T(8,128)(2,1)}), bf16[16,72,384]{2,1,0:T(8,128)(2,1)S(1)}, u32[]{:S(2)}, u32[]{:S(2)}) async-start(bf16[16,72,384]{2,1,0:T(8,128)(2,1)} %pad_maximum_fusion.1), calls=%async_computation | async-start | bytes 1769472 | tf_op jit(solution)/shard_map/all_to_all | solution.py:387
  80.7 32.0 %all-to-all-done = bf16[16,72,384]{2,1,0:T(8,128)(2,1)S(1)} async-done(((bf16[16,72,384]{2,1,0:T(8,128)(2,1)}), bf16[16,72,384]{2,1,0:T(8,128)(2,1)S(1)}, u32[]{:S(2)}, u32[]{:S(2)}) %all-to-all-start) | async-done | bytes 884768 | tf_op jit(solution)/shard_map/all_to_all | solution.py:387
  117.4 2.5 maximum_select_fusion
  120.6 12.4 %collective-permute-done.3 = bf16[16,64,384]{2,1,0:T(8,128)(2,1)} collective-permute-done((bf16[16,64,384]{2,1,0:T(8,128)(2,1)}, bf16[16,64,384]{2,1,0:T(8,128)(2,1)}, u32[]{:S(2)}, u32[]{:S(2)}) %collective-permute-start.3) | collective-permute-done | bytes 786464 | tf_op jit(solution)/shard_map/ppermute | solution.py:47
  140.3 19.5 %norm_up_qkv.1 = (bf16[1024,2048]{1,0:T(8,128)(2,1)}, bf16[1024,2048]{1,0:T(8,128)(2,1)}, bf16[1024,512]{1,0:T(8,128)(2,1)}, bf16[1024,512]{1,0:T(8,128)(2,1)}, ...) custom-call(bf16[1024,2048]{1,0:T(8,128)(2,1)} %all-gather.3.cloned., ...), custom_call_target="tpu_custom_call" | custom-call | flops 7516192768 | bytes 30977024 | tf_op jit(solution)/shard_map/norm_up_qkv/pallas_call | solution.py:168
  159.8 4.8 %attend.1 = (bf16[1024,256]{1,0:T(8,128)(2,1)}, f32[1024,1]{1,0:T(8,128)}) custom-call(bf16[1024,256]{1,0:T(8,128)(2,1)} %get-tuple-element.47.refs_0_, bf16[1024,256]{1,0:T(8,128)(2,1)} %get-tuple-element.48.refs_1_, bf16[1024,256]{1,0:T(8,128)(2,1)} %get-tuple-element.49.refs_2_, f32[1024,1]{1,0:T(8,128)} %compare_convert_fusion.refs_1_.refs_3_, ...), custom_call_target="tpu_custom_call" | custom-call | flops 1073741824 | bytes 2113536 | tf_op jit(solution)/shard_map/attend/pallas_call | solution.py:168
  164.6 10.1 %dense_down.1 = (bf16[1024,2048]{1,0:T(8,128)(2,1)}, f32[8,128]{1,0:T(8,128)}) custom-call(bf16[1024,512]{1,0:T(8,128)(2,1)} %get-tuple-element.45.refs_0_, bf16[1024,512]{1,0:T(8,128)(2,1)} %get-tuple-element.46.refs_1_.refs_0_, bf16[1024,256]{1,0:T(8,128)(2,1)} %get-tuple-element.50.refs_2_.refs_0_, bf16[512,2048]{1,0:T(8,128)(2,1)} %refs_4_.1, ...), custom_call_target="tpu_custom_call" | custom-call | flops 5368709120 | bytes 12062720 | tf_op jit(solution)/shard_map/dense_down/pallas_call | solution.py:168
  174.8 18.1 %all-gather.5.cloned.1.call-done.refs_0_.refs_1_ = bf16[1024,2048]{1,0:T(8,128)(2,1)} async-done(((bf16[128,2048]{1,0:T(8,128)(2,1)}), bf16[1024,2048]{1,0:T(8,128)(2,1)}) %all-gather.5.cloned.1.call-update) | async-done | bytes 4194320 | tf_op jit(solution)/shard_map/all_gather | solution.py:70
  192.9 10.7 %back_dense_down.1 = (bf16[1024,512]{1,0:T(8,128)(2,1)}, bf16[1024,512]{1,0:T(8,128)(2,1)}, bf16[1024,256]{1,0:T(8,128)(2,1)}, f32[2,512]{1,0:T(2,128)}, f32[1,2048]{1,0:T(1,128)}) custom-call(bf16[1024,2048]{1,0:T(8,128)(2,1)} %all-gather.5.cloned.1.call-done.refs_0_.refs_1_, f32[1024,1]{1,0:T(8,128)} %compare_convert_fusion.refs_1_.refs_3_, ...), custom_call_target="tpu_custom_call" | custom-call | flops 5368709120 | bytes 16269312 | tf_op jit(solution)/shard_map/back_dense_down/pallas_call | solution.py:168
  203.6 8.2 %grad_up_other.1.refs_10_ = bf16[2048,512]{1,0:T(8,128)(2,1)} custom-call(bf16[1024,2048]{1,0:T(8,128)(2,1)} %get-tuple-element.57.refs_0_.refs_1_, bf16[1024,512]{1,0:T(8,128)(2,1)} %get-tuple-element.58.refs_1_.refs_3_), custom_call_target="tpu_custom_call" | custom-call | flops 2147483648 | bytes 7340032 | tf_op jit(solution)/shard_map/grad_up_other/pallas_call | solution.py:168
  214.3 7.9 %back_attend.1 = (bf16[1024,384]{1,0:T(8,128)(2,1)}, bf16[1024,384]{1,0:T(8,128)(2,1)}, f32[2,384]{1,0:T(2,128)}) custom-call(bf16[1024,256]{1,0:T(8,128)(2,1)} %get-tuple-element.47.refs_0_, bf16[1024,256]{1,0:T(8,128)(2,1)} %get-tuple-element.48.refs_1_, bf16[1024,256]{1,0:T(8,128)(2,1)} %get-tuple-element.49.refs_2_, ...), custom_call_target="tpu_custom_call" | custom-call | flops 2684354560 | bytes 6831104 | tf_op jit(solution)/shard_map/back_attend/pallas_call | solution.py:168
  224.2 9.0 %grad_up_own.1 = (bf16[16,64,512]{2,1,0:T(8,128)(2,1)}, bf16[16,64,512]{2,1,0:T(8,128)(2,1)}) custom-call(s32[1]{0:T(128)} %bitcast.22.refs_0_, bf16[1024,2048]{1,0:T(8,128)(2,1)} %get-tuple-element.57.refs_0_.refs_1_, bf16[1024,512]{1,0:T(8,128)(2,1)} %get-tuple-element.61.refs_2_, bf16[2048,512]{1,0:T(8,128)(2,1)} %copy-done.12, ...), custom_call_target="tpu_custom_call" | custom-call | flops 2147483648 | bytes 9437188 | tf_op jit(solution)/shard_map/grad_up_own/pallas_call | solution.py:168
  234.4 8.0 %grad_qkv_other.1.refs_2_ = bf16[2048,384]{1,0:T(8,128)(2,1)} custom-call(bf16[1024,2048]{1,0:T(8,128)(2,1)} %get-tuple-element.62.refs_0_.refs_1_, bf16[1024,384]{1,0:T(8,128)(2,1)} %get-tuple-element.60.refs_1_, bf16[16,64,512]{2,1,0:T(8,128)(2,1)} %get-tuple-element.65.refs_2_.refs_0_), custom_call_target="tpu_custom_call" | custom-call | flops 1610612736 | bytes 6553600 | tf_op jit(solution)/shard_map/grad_qkv_other/pallas_call | solution.py:168
  242.4 3.8 grad_down_other.1.refs_3_
  250.2 3.9 grad_down_own.1.refs_2_
  254.2 5.8 %grad_down_other2.1.refs_3_ = bf16[384,2048]{1,0:T(8,128)(2,1)} custom-call(bf16[1024,512]{1,0:T(8,128)(2,1)} %get-tuple-element.46.refs_1_.refs_0_, bf16[1024,2048]{1,0:T(8,128)(2,1)} %all-gather.5.cloned.1.call-done.refs_0_.refs_1_, bf16[128,2048]{1,0:T(8,128)(2,1)} %grad_down_own.1.refs_2_), custom_call_target="tpu_custom_call" | custom-call | flops 1610612736 | bytes 6815744 | tf_op jit(solution)/shard_map/grad_down_other2/pallas_call | solution.py:168
  261.0 2.8 half_up.1.refs_4_
  263.8 5.5 %all-to-all-start.2 = ((bf16[16,72,512]{2,1,0:T(8,128)(2,1)}), bf16[16,72,512]{2,1,0:T(8,128)(2,1)S(1)}, u32[]{:S(2)}, u32[]{:S(2)}) async-start(bf16[16,72,512]{2,1,0:T(8,128)(2,1)} %half_up.1.refs_4_), calls=%async_computation.3 | async-start | bytes 2359296 | tf_op jit(solution)/shard_map/all_to_all | solution.py:579
  271.9 8.4 %grad_qkv_own.1 = (bf16[16,64,384]{2,1,0:T(8,128)(2,1)}, bf16[16,64,384]{2,1,0:T(8,128)(2,1)}) custom-call(s32[1]{0:T(128)} %bitcast.22.refs_0_, bf16[1024,2048]{1,0:T(8,128)(2,1)} %get-tuple-element.62.refs_0_.refs_1_, bf16[1024,384]{1,0:T(8,128)(2,1)} %get-tuple-element.59.refs_4_.refs_2_.refs_0_, bf16[2048,384]{1,0:T(8,128)(2,1)} %collective-permute-done.11.refs_3_, ...), custom_call_target="tpu_custom_call" | custom-call | flops 1610612736 | bytes 8126468 | tf_op jit(solution)/shard_map/grad_qkv_own/pallas_call | solution.py:168
  283.4 14.3 %back_up_qkv.1 = (bf16[1024,2048]{1,0:T(8,128)(2,1)}, f32[8,128]{1,0:T(8,128)}) custom-call(bf16[1024,384]{1,0:T(8,128)(2,1)} %get-tuple-element.59.refs_4_.refs_2_.refs_0_, bf16[1024,384]{1,0:T(8,128)(2,1)} %get-tuple-element.60.refs_1_, bf16[1024,512]{1,0:T(8,128)(2,1)} %get-tuple-element.61.refs_2_, bf16[1024,512]{1,0:T(8,128)(2,1)} %get-tuple-element.58.refs_1_.refs_3_, ...), custom_call_target="tpu_custom_call" | custom-call | flops 7516192768 | bytes 15241216 | tf_op jit(solution)/shard_map/back_up_qkv/pallas_call | solution.py:168
  302.9 6.5 %all-to-all-done.2.refs_3_.refs_1_ = bf16[16,72,512]{2,1,0:T(8,128)(2,1)S(1)} async-done(((bf16[16,72,512]{2,1,0:T(8,128)(2,1)}), bf16[16,72,512]{2,1,0:T(8,128)(2,1)S(1)}, u32[]{:S(2)}, u32[]{:S(2)}) %all-to-all-start.2) | async-done | bytes 1179680 | tf_op jit(solution)/shard_map/all_to_all | solution.py:579
  312.3 3.8 grad_dense_other.1.refs_3_
  316.2 6.4 %grad_down_own2.1.refs_3_ = bf16[384,2048]{1,0:T(8,128)(2,1)} custom-call(bf16[1024,512]{1,0:T(8,128)(2,1)} %get-tuple-element.45.refs_0_, bf16[1024,2048]{1,0:T(8,128)(2,1)} %all-gather.5.cloned.1.call-done.refs_0_.refs_1_, bf16[384,2048]{1,0:T(8,128)(2,1)} %collective-permute-done.20.refs_2_, bf16[128,2048]{1,0:T(8,128)(2,1)} %grad_dense_other.1.refs_3_), custom_call_target="tpu_custom_call" | custom-call | flops 1610612736 | bytes 8388608 | tf_op jit(solution)/shard_map/grad_down_own2/pallas_call | solution.py:168
  323.9 5.3 %all-to-all-start.3 = ((bf16[16,72,384]{2,1,0:T(8,128)(2,1)}), bf16[16,72,384]{2,1,0:T(8,128)(2,1)S(1)}, u32[]{:S(2)}, u32[]{:S(2)}) async-start(bf16[16,72,384]{2,1,0:T(8,128)(2,1)} %gate.7), calls=%async_computation.5 | async-start | bytes 1769472 | tf_op jit(solution)/shard_map/all_to_all | solution.py:657
  330.2 4.0 grad_dense_own.1
  336.4 58.6 %collective-permute-done.21 = bf16[128,2048]{1,0:T(8,128)(2,1)S(1)} collective-permute-done((bf16[128,2048]{1,0:T(8,128)(2,1)}, bf16[128,2048]{1,0:T(8,128)(2,1)S(1)}, u32[]{:S(2)}, u32[]{:S(2)}) %collective-permute-start.21) | collective-permute-done | bytes 524320 | tf_op jit(solution)/shard_map/ppermute | solution.py:47
  401.1 5.2 %rows_up.1 = (f32[128,8192]{1,0:T(8,128)}, f32[128,2]{1,0:T(8,128)}) custom-call(s32[1]{0:T(128)} %bitcast.22.refs_0_, bf16[16,72,512]{2,1,0:T(8,128)(2,1)} %copy-done, bf16[16,72,512]{2,1,0:T(8,128)(2,1)} %copy-done.15, bf16[128,8192]{1,0:T(8,128)(2,1)} %refs_3_.5, bf16[16,72,384]{2,1,0:T(8,128)(2,1)} %copy-done.2), custom_call_target="tpu_custom_call" | custom-call | bytes 8651780 | tf_op jit(solution)/shard_map/rows_up/pallas_call | solution.py:168
  410.0 2.5 pad_maximum_fusion
  413.0 7.9 %collective-permute-done.18.refs_2_.refs_1_ = bf16[16,72,384]{2,1,0:T(8,128)(2,1)} collective-permute-done((bf16[16,72,384]{2,1,0:T(8,128)(2,1)}, bf16[16,72,384]{2,1,0:T(8,128)(2,1)}, u32[]{:S(2)}, u32[]{:S(2)}) %collective-permute-start.18) | collective-permute-done | bytes 884768 | tf_op jit(solution)/shard_map/ppermute | solution.py:47
  420.9 5.1 %rows_qkv.1 = (f32[128,6144]{1,0:T(8,128)}, f32[128,2]{1,0:T(8,128)}) custom-call(s32[1]{0:T(128)} %bitcast.22.refs_0_, bf16[16,72,384]{2,1,0:T(8,128)(2,1)} %copy-done.2, bf16[16,72,384]{2,1,0:T(8,128)(2,1)} %collective-permute-done.18.refs_2_.refs_1_, bf16[128,6144]{1,0:T(8,128)(2,1)} %refs_3_.4), custom_call_target="tpu_custom_call" | custom-call | bytes 6489092 | tf_op jit(solution)/shard_map/rows_qkv/pallas_call | solution.py:168
  (253 shorter events, 97.0 us)
Async XLA Ops:
  7.2 133.1 %all-gather.3.cloned.1.call-start = ((), (), s32[]{:S(2)}) async-start(), calls=%async_computation.6 | async-start | bytes 4718592 | tf_op jit(solution)/shard_map/all_gather | solution.py:70
  8.5 1.9 collective-permute-start
  16.3 46.6 %all-to-all-start.1 = ((bf16[16,64,512]{2,1,0:T(8,128)(2,1)}), bf16[16,64,512]{2,1,0:T(8,128)(2,1)}, u32[]{:S(2)}, u32[]{:S(2)}) async-start(bf16[16,64,512]{2,1,0:T(8,128)(2,1)} %bitcast.94), calls=%async_computation.1 | async-start | bytes 2097152 | tf_op jit(solution)/shard_map/all_to_all | solution.py:382
  22.7 170.2 %all-gather.5.cloned.1.call-start = ((), (), s32[]{:S(2)}) async-start(), calls=%async_computation.8 | async-start | bytes 4718592 | tf_op jit(solution)/shard_map/all_gather | solution.py:70
  22.8 1.6 collective-permute-start.8
  23.2 92.1 %collective-permute-start.6 = (bf16[128,2048]{1,0:T(8,128)(2,1)}, bf16[128,2048]{1,0:T(8,128)(2,1)}, u32[]{:S(2)}, u32[]{:S(2)}) collective-permute-start(bf16[128,2048]{1,0:T(8,128)(2,1)} %param.21), channel_id=1, source_target_pairs={{0,1},{1,0},{2,3},{3,2},{4,5},{5,4},{6,7},{7,6},{8,9},{9,8},{10,11... | collective-permute-start | bytes 1572872 | tf_op jit(solution)/shard_map/ppermute | solution.py:47
  23.4 141.2 %collective-permute-start.5 = (bf16[512,2048]{1,0:T(8,128)(2,1)}, bf16[512,2048]{1,0:T(8,128)(2,1)}, u32[]{:S(2)}, u32[]{:S(2)}) collective-permute-start(bf16[512,2048]{1,0:T(8,128)(2,1)} %refs_4_.1), channel_id=1, source_target_pairs={{0,1},{1,0},{2,3},{3,2},{4,5},{5,4},{6,7},{7,6},{8,9},{9,8},{10,11... | collective-permute-start | bytes 6291464 | tf_op jit(solution)/shard_map/ppermute | solution.py:47
  62.9 49.8 %all-to-all-start = ((bf16[16,72,384]{2,1,0:T(8,128)(2,1)}), bf16[16,72,384]{2,1,0:T(8,128)(2,1)S(1)}, u32[]{:S(2)}, u32[]{:S(2)}) async-start(bf16[16,72,384]{2,1,0:T(8,128)(2,1)} %pad_maximum_fusion.1), calls=%async_computation | async-start | bytes 1769472 | tf_op jit(solution)/shard_map/all_to_all | solution.py:387
  67.6 241.8 %reduce-scatter.3.cloned.1.call-start = ((), (), s32[]{:S(2)}) async-start(), calls=%async_computation.7 | async-start | bytes 4718592 | tf_op jit(solution)/shard_map/reduce_scatter | solution.py:148
  76.2 41.1 %collective-permute-start.1 = (bf16[16,64,512]{2,1,0:T(8,128)(2,1)}, bf16[16,64,512]{2,1,0:T(8,128)(2,1)}, u32[]{:S(2)}, u32[]{:S(2)}) collective-permute-start(bf16[16,64,512]{2,1,0:T(8,128)(2,1)} %all-to-all-done.1), channel_id=1, source_target_pairs={{0,16},{16,0},{1,17},{17,1},{2,18},{18,2},{3,19},{19,3},{4,20},{20... | collective-permute-start | bytes 3145736 | tf_op jit(solution)/shard_map/ppermute | solution.py:47
  113.9 19.2 %collective-permute-start.3 = (bf16[16,64,384]{2,1,0:T(8,128)(2,1)}, bf16[16,64,384]{2,1,0:T(8,128)(2,1)}, u32[]{:S(2)}, u32[]{:S(2)}) collective-permute-start(bf16[16,64,384]{2,1,0:T(8,128)(2,1)} %get-tuple-element.87), channel_id=1, source_target_pairs={{0,16},{16,0},{1,17},{17,1},{2,18},{18,2},{3,19},{19,3},{4,20},{20... | collective-permute-start | bytes 2359304 | tf_op jit(solution)/shard_map/ppermute | solution.py:47
  119.9 20.4 %collective-permute-start.2 = (bf16[2048,512]{1,0:T(8,128)(2,1)S(1)}, bf16[2048,512]{1,0:T(8,128)(2,1)}, u32[]{:S(2)}, u32[]{:S(2)}) collective-permute-start(bf16[2048,512]{1,0:T(8,128)(2,1)S(1)} %bitcast.96), channel_id=1, source_target_pairs={{0,1},{1,0},{2,3},{3,2},{4,5},{5,4},{6,7},{7,6},{8,9},{9,8},{10,11... | collective-permute-start | bytes 6291464 | tf_op jit(solution)/shard_map/ppermute | solution.py:47
  134.9 4.2 collective-permute-start.4
  211.7 11.1 %collective-permute-start.9 = (bf16[2048,512]{1,0:T(8,128)(2,1)}, bf16[2048,512]{1,0:T(8,128)(2,1)S(1)}, u32[]{:S(2)}, u32[]{:S(2)}) collective-permute-start(bf16[2048,512]{1,0:T(8,128)(2,1)} %grad_up_other.1.refs_10_), channel_id=1, source_target_pairs={{0,1},{1,0},{2,3},{3,2},{4,5},{5,4},{6,7},{7,6},{8,9},{9,8},{10,11... | collective-permute-start | bytes 6291464 | tf_op jit(solution)/shard_map/ppermute | solution.py:47
  214.2 8.0 %collective-permute-start.10 = (f32[640]{0:T(1024)S(1)}, f32[640]{0:T(1024)S(1)}, u32[]{:S(2)}, u32[]{:S(2)}) collective-permute-start(f32[640]{0:T(1024)S(1)} %pad_maximum_fusion.5), channel_id=1, source_target_pairs={{0,1},{1,0},{2,3},{3,2},{4,5},{5,4},{6,7},{7,6},{8,9},{9,8},{10,11... | collective-permute-start | bytes 7688 | tf_op jit(solution)/shard_map/ppermute | solution.py:47
  233.2 26.8 %collective-permute-start.12 = (bf16[16,64,512]{2,1,0:T(8,128)(2,1)}, bf16[16,64,512]{2,1,0:T(8,128)(2,1)S(1)}, u32[]{:S(2)}, u32[]{:S(2)}) collective-permute-start(bf16[16,64,512]{2,1,0:T(8,128)(2,1)} %get-tuple-element.66), channel_id=1, source_target_pairs={{0,16},{16,0},{1,17},{17,1},{2,18},{18,2},{3,19},{19,3},{4,20},{20... | collective-permute-start | bytes 3145736 | tf_op jit(solution)/shard_map/ppermute | solution.py:47
  246.2 3.2 collective-permute-start.13
  247.0 24.9 %collective-permute-start.11 = (bf16[2048,384]{1,0:T(8,128)(2,1)}, bf16[2048,384]{1,0:T(8,128)(2,1)}, u32[]{:S(2)}, u32[]{:S(2)}) collective-permute-start(bf16[2048,384]{1,0:T(8,128)(2,1)} %grad_qkv_other.1.refs_2_), channel_id=1, source_target_pairs={{0,1},{1,0},{2,3},{3,2},{4,5},{5,4},{6,7},{7,6},{8,9},{9,8},{10,11... | collective-permute-start | bytes 4718600 | tf_op jit(solution)/shard_map/ppermute | solution.py:47
  263.8 45.7 %all-to-all-start.2 = ((bf16[16,72,512]{2,1,0:T(8,128)(2,1)}), bf16[16,72,512]{2,1,0:T(8,128)(2,1)S(1)}, u32[]{:S(2)}, u32[]{:S(2)}) async-start(bf16[16,72,512]{2,1,0:T(8,128)(2,1)} %half_up.1.refs_4_), calls=%async_computation.3 | async-start | bytes 2359296 | tf_op jit(solution)/shard_map/all_to_all | solution.py:579
  269.3 159.5 %reduce-scatter.5.cloned.1.call-start = ((), (), s32[]{:S(2)}) async-start(), calls=%async_computation.9 | async-start | bytes 4718592 | tf_op jit(solution)/shard_map/reduce_scatter | solution.py:148
  269.3 13.2 %collective-permute-start.15 = (bf16[128,2048]{1,0:T(8,128)(2,1)S(1)}, bf16[128,2048]{1,0:T(8,128)(2,1)S(1)}, u32[]{:S(2)}, u32[]{:S(2)}) collective-permute-start(bf16[128,2048]{1,0:T(8,128)(2,1)S(1)} %copy-done.7), channel_id=1, source_target_pairs={{0,16},{16,0},{1,17},{17,1},{2,18},{18,2},{3,19},{19,3},{4,20},{20... | collective-permute-start | bytes 1572872 | tf_op jit(solution)/shard_map/ppermute | solution.py:47
  280.3 19.3 %collective-permute-start.16 = (bf16[16,64,384]{2,1,0:T(8,128)(2,1)}, bf16[16,64,384]{2,1,0:T(8,128)(2,1)S(1)}, u32[]{:S(2)}, u32[]{:S(2)}) collective-permute-start(bf16[16,64,384]{2,1,0:T(8,128)(2,1)} %get-tuple-element.70), channel_id=1, source_target_pairs={{0,16},{16,0},{1,17},{17,1},{2,18},{18,2},{3,19},{19,3},{4,20},{20... | collective-permute-start | bytes 2359304 | tf_op jit(solution)/shard_map/ppermute | solution.py:47
  311.9 4.3 collective-permute-start.20
  316.1 14.1 %collective-permute-start.19 = (bf16[128,2048]{1,0:T(8,128)(2,1)}, bf16[128,2048]{1,0:T(8,128)(2,1)}, u32[]{:S(2)}, u32[]{:S(2)}) collective-permute-start(bf16[128,2048]{1,0:T(8,128)(2,1)} %grad_dense_other.1.refs_3_), channel_id=1, source_target_pairs={{0,1},{1,0},{2,3},{3,2},{4,5},{5,4},{6,7},{7,6},{8,9},{9,8},{10,11... | collective-permute-start | bytes 1572872 | tf_op jit(solution)/shard_map/ppermute | solution.py:47
  322.6 83.7 %collective-permute-start.24 = (bf16[384,2048]{1,0:T(8,128)(2,1)}, bf16[384,2048]{1,0:T(8,128)(2,1)}, u32[]{:S(2)}, u32[]{:S(2)}) collective-permute-start(bf16[384,2048]{1,0:T(8,128)(2,1)} %grad_down_own2.1.refs_3_), channel_id=1, source_target_pairs={{0,16},{16,0},{1,17},{17,1},{2,18},{18,2},{3,19},{19,3},{4,20},{20... | collective-permute-start | bytes 4718600 | tf_op jit(solution)/shard_map/ppermute | solution.py:47
  323.9 74.8 %all-to-all-start.3 = ((bf16[16,72,384]{2,1,0:T(8,128)(2,1)}), bf16[16,72,384]{2,1,0:T(8,128)(2,1)S(1)}, u32[]{:S(2)}, u32[]{:S(2)}) async-start(bf16[16,72,384]{2,1,0:T(8,128)(2,1)} %gate.7), calls=%async_computation.5 | async-start | bytes 1769472 | tf_op jit(solution)/shard_map/all_to_all | solution.py:657
  330.0 67.1 %collective-permute-start.23 = (bf16[16,72,512]{2,1,0:T(8,128)(2,1)S(1)}, bf16[16,72,512]{2,1,0:T(8,128)(2,1)S(1)}, u32[]{:S(2)}, u32[]{:S(2)}) collective-permute-start(bf16[16,72,512]{2,1,0:T(8,128)(2,1)S(1)} %copy-done.1), channel_id=1, source_target_pairs={{0,16},{16,0},{1,17},{17,1},{2,18},{18,2},{3,19},{19,3},{4,20},{20... | collective-permute-start | bytes 3538952 | tf_op jit(solution)/shard_map/ppermute | solution.py:47
  334.1 60.8 %collective-permute-start.21 = (bf16[128,2048]{1,0:T(8,128)(2,1)}, bf16[128,2048]{1,0:T(8,128)(2,1)S(1)}, u32[]{:S(2)}, u32[]{:S(2)}) collective-permute-start(bf16[128,2048]{1,0:T(8,128)(2,1)} %grad_dense_own.1), channel_id=1, source_target_pairs={{0,16},{16,0},{1,17},{17,1},{2,18},{18,2},{3,19},{19,3},{4,20},{20... | collective-permute-start | bytes 1572872 | tf_op jit(solution)/shard_map/ppermute | solution.py:47
  399.6 26.3 %collective-permute-start.22 = (f32[128]{0:T(128)}, f32[128]{0:T(128)S(1)}, u32[]{:S(2)}, u32[]{:S(2)}) collective-permute-start(f32[128]{0:T(128)} %gate.8), channel_id=1, source_target_pairs={{0,16},{16,0},{1,17},{17,1},{2,18},{18,2},{3,19},{19,3},{4,20},{20... | collective-permute-start | bytes 1544 | tf_op jit(solution)/shard_map/ppermute | solution.py:47
  400.9 20.0 %collective-permute-start.18 = (bf16[16,72,384]{2,1,0:T(8,128)(2,1)}, bf16[16,72,384]{2,1,0:T(8,128)(2,1)}, u32[]{:S(2)}, u32[]{:S(2)}) collective-permute-start(bf16[16,72,384]{2,1,0:T(8,128)(2,1)} %copy-done.2), channel_id=1, source_target_pairs={{0,16},{16,0},{1,17},{17,1},{2,18},{18,2},{3,19},{19,3},{4,20},{20... | collective-permute-start | bytes 2654216 | tf_op jit(solution)/shard_map/ppermute | solution.py:47
  432.0 4.3 collective-permute-start.17
  434.6 2.7 collective-permute-start.7
  (42 other events, 315.9 us)
Sparse Core Ops, SparseCore 0:
  11.3 106.5 all-gather.2
  120.0 72.7 all-gather.4
  196.5 105.9 reduce-scatter.2
  310.6 107.4 reduce-scatter.4
